TPU v7x, 512 devices: a whole 4x4x16 slice. The times are simulated.
512 devices in a mesh: vocab: 128 (over y, z, core), tok: 4 (over x).
Axes of the slice: x: 4, y: 4, z: 16, core: 2. Of those that a mesh axis runs over, the one named last changes fastest.
Arguments:
- hidden: bfloat16 [512, 16384], P('vocab', 'tok'), may hold values from -5.5 to 5.5
- head: bfloat16 [16384, 65536], P('tok', 'vocab'), may hold values from -1 to 1
- targets: int32 [512], replicated, may hold values from 0 to 65535
- segment_ids: int32 [512], replicated, may hold values from 0 to 7, never falling along the last dimension, each value on 1 to 128 neighbouring positions
- grad_slab: bfloat16 [65536, 64], P('vocab'), may hold values from -6 to 6
- feature_slab: bfloat16 [16384, 64], P('tok'), may hold values from -0.046875 to 0.046875
Outputs:
- sketch: float32 [8, 4096], replicated
All inputs are finite; a program needn't handle non-finite values.
Results may differ from a plain program's by a relative error of at most 0.0016.
Values may be sent and summed in bfloat16 or wider, within the bound.
No kernel may reach another device: no remote copies, remote signals or barrier semaphores. Data moves between devices by JAX's collectives and lax.ppermute only.
A program may use at most 64 MiB of HBM per device.

v0:
```python
import jax
import jax.numpy as jnp
from jax import lax
from jax.sharding import PartitionSpec as P


def gradient(logits, row_targets, col_offset):
    local_top = jnp.max(logits, axis=1)
    row_top = lax.pmax(local_top, "vocab")
    exponent = jnp.exp(logits - row_top[:, None])
    row_sum = lax.psum(jnp.sum(exponent, axis=1), "vocab")
    column = lax.broadcasted_iota(jnp.int32, logits.shape, 1) + col_offset
    onehot = (column == row_targets[:, None]).astype(jnp.float32)
    return (exponent / row_sum[:, None] - onehot).astype(jnp.bfloat16)


def on_device(hidden, head, targets, segment_ids, grad_slab, feature_slab):
    n_vocab = lax.axis_size("vocab")
    n_tok = lax.axis_size("tok")
    vocab_index = lax.axis_index("vocab")
    tok_index = lax.axis_index("tok")
    tokens = targets.shape[0]
    shard_cols = head.shape[1]
    sketch_width = feature_slab.shape[1]
    owned_rows = tokens // (n_vocab * n_tok)
    documents = tokens // 64
    partial_logits = jnp.dot(
        lax.all_gather(hidden, "vocab", axis=0, tiled=True),
        head,
        preferred_element_type=jnp.float32,
    )
    group_rows = tokens // n_tok
    summed = lax.psum_scatter(
        partial_logits.reshape(group_rows, n_tok, shard_cols),
        "tok",
        scatter_dimension=1,
        tiled=True,
    )
    logits = summed.reshape(group_rows, shard_cols)
    row_targets = lax.dynamic_slice_in_dim(
        targets.reshape(group_rows, n_tok), tok_index, 1, 1
    ).reshape(group_rows)
    grad_rows = gradient(logits, row_targets, vocab_index * shard_cols)
    grad_sketch = lax.psum_scatter(
        jnp.dot(grad_rows, grad_slab, preferred_element_type=jnp.float32),
        "vocab",
        scatter_dimension=0,
        tiled=True,
    )
    quarter = jnp.dot(hidden, feature_slab, preferred_element_type=jnp.float32)
    feat_parts = lax.psum_scatter(
        quarter.reshape(owned_rows, n_tok, sketch_width), "tok", scatter_dimension=1, tiled=True
    )
    feat_sketch = feat_parts.reshape(owned_rows, sketch_width)
    doc_index = lax.broadcasted_iota(jnp.int32, (1, documents), 1)
    member_all = (segment_ids[:, None] == doc_index).astype(jnp.float32)
    counts = jnp.sum(member_all, axis=0)
    inverse_root = 1.0 / jnp.sqrt(counts)
    segs_cube = segment_ids.reshape(n_vocab, owned_rows, n_tok)
    local_segs = lax.dynamic_slice(
        segs_cube, (vocab_index, 0, tok_index), (1, owned_rows, 1)
    ).reshape(owned_rows)
    member_local = (local_segs[:, None] == doc_index).astype(jnp.float32)
    outer_rows = (grad_sketch[:, :, None] * feat_sketch[:, None, :]).reshape(
        owned_rows, sketch_width * sketch_width
    )
    partial_docs = jnp.dot(member_local.T, outer_rows, precision=lax.Precision.HIGHEST)
    summed_docs = lax.psum(partial_docs, ("vocab", "tok"))
    return summed_docs * inverse_root[:, None]


def solution(mesh):
    return jax.shard_map(
        on_device,
        mesh=mesh,
        in_specs=(P("vocab", "tok"), P("tok", "vocab"), P(), P(), P("vocab", None), P("tok", None)),
        out_specs=P(),
        check_vma=False,
    )
```

profile of v0, /device:TPU:1, one launch (start us, length us, event | category | flops | bytes accessed | tf_op | source)
XLA Modules:
  0.0 1637.1 jit_solution(5897678762915626829)
XLA Ops:
  6.5 0.0 copy-start
  6.5 0.0 all-gather.3.cloned.1.call-start
  6.5 0.7 all-gather.3.cloned.1.call-update
  7.3 0.0 reduce-scatter.3.cloned.1.call-start
  7.3 151.0 %all-gather.3.cloned.1.call-done = bf16[128,4,4096]{2,1,0:T(4,128)(2,1)} async-done(((bf16[1,4,4096]{2,1,0:T(4,128)(2,1)}), bf16[128,4,4096]{2,1,0:T(4,128)(2,1)}) %all-gather.3.cloned.1.call-update) | async-done | bytes 4194320 | tf_op jit(solution)/shard_map/all_gather | solution.py:28
  158.3 6.9 reshape.128
  165.2 5.8 fusion.6
  171.0 0.0 copy-start.3
  171.0 0.0 copy-start.2
  171.0 0.0 copy-start.1
  171.0 0.0 copy-start.4
  171.1 0.3 reshape.122
  171.4 1.3 copy.8
  172.7 0.0 reduce-scatter.3.cloned.1.call-update
  172.7 0.0 all-reduce.4.cloned.1.call-start
  172.8 0.0 copy-done.3
  172.8 0.1 reshape.124
  172.9 1.3 dynamic-slice.2
  174.2 1.3 dynamic-slice
  175.5 0.0 copy-done.2
  175.5 0.1 reshape.120
  175.6 0.6 constant_dynamic-slice_fusion.2
  176.2 0.2 dynamic-slice_reduce_fusion
  176.4 0.0 copy-done
  176.4 0.0 copy-done.1
  176.4 0.2 convolution_bitcast_fusion
  176.6 8.4 all-reduce.1
  185.0 0.6 fusion.5
  185.6 0.7 fusion.4
  186.3 11.1 reduce-scatter.3.cloned.1.call-done
  197.4 1.1 reduce_max.9
  198.5 250.2 %pmax.7 = f32[128]{0:T(128)S(1)} all-reduce(f32[128]{0:T(128)S(1)} %reduce_max.9), channel_id=1, replica_groups=mesh['vocab'=128,'tok'=4] {'vocab'}, use_global_device_ids=true, to_apply=%region_2.0 | all-reduce | flops 128 | bytes 1024 | tf_op jit(solution)/shard_map/pmax | solution.py:9
  448.7 1.1 fusion.1
  449.8 249.8 %psum.14 = f32[128]{0:T(128)S(1)} all-reduce(f32[128]{0:T(128)S(1)} %fusion.1), channel_id=1, replica_groups=mesh['vocab'=128,'tok'=4] {'vocab'}, use_global_device_ids=true, to_apply=%region_4.0 | all-reduce | flops 128 | bytes 1024 | tf_op jit(solution)/shard_map/psum | solution.py:11
  699.6 0.0 copy-done.4
  699.6 1.2 fusion.2
  700.8 485.9 %all-reduce = f32[128,64]{1,0:T(8,128)S(1)} all-reduce(f32[128,64]{1,0:T(8,128)S(1)} %fusion.2), channel_id=3, replica_groups=mesh['vocab'=128,'tok'=4] {'vocab'}, use_global_device_ids=true, to_apply=%region_5.0.clone | all-reduce | flops 8192 | bytes 65536
  1186.7 0.6 fusion.3
  1187.3 0.2 multiply_reduce_fusion
  1187.5 0.1 mul.47
  1187.6 0.7 broadcast_multiply_fusion.1
  1188.3 0.0 all-reduce.4.cloned.1.call-update
  1188.3 0.1 convert_reduce_fusion
  1188.5 440.5 %all-reduce.4.cloned.1.call-done = f32[8,4096]{1,0:T(8,128)} async-done(((f32[8,4096]{1,0:T(8,128)}), f32[8,4096]{1,0:T(8,128)}) %all-reduce.4.cloned.1.call-update) | async-done | bytes 131088 | tf_op jit(solution)/shard_map/psum | solution.py:68
  1628.9 1.6 broadcast_multiply_fusion
  (2 shorter events, 0.0 us)
Async XLA Ops:
  6.5 169.8 %copy-start = (bf16[4096,64]{0,1:T(8,128)(2,1)S(1)}, bf16[4096,64]{0,1:T(8,128)(2,1)}, u32[]{:S(2)}) copy-start(bf16[4096,64]{0,1:T(8,128)(2,1)} %param.11) | copy-start | bytes 1572868
  6.5 151.8 %all-gather.3.cloned.1.call-start = ((), (), s32[]{:S(2)}) async-start(), calls=%async_computation.3 | async-start | bytes 4227072 | tf_op jit(solution)/shard_map/all_gather | solution.py:28
  7.3 190.2 %reduce-scatter.3.cloned.1.call-start = ((), (), s32[]{:S(2)}) async-start(), calls=%async_computation.1 | async-start | bytes 1310720 | tf_op jit(solution)/shard_map/reduce_scatter | solution.py:33
  171.0 1.8 copy-start.3
  171.0 4.4 copy-start.2
  171.0 5.3 copy-start.1
  171.0 528.6 %copy-start.4 = (bf16[512,64]{0,1:T(8,128)(2,1)S(1)}, bf16[512,64]{0,1:T(8,128)(2,1)}, u32[]{:S(2)}) copy-start(bf16[512,64]{0,1:T(8,128)(2,1)} %param.10) | copy-start | bytes 196612
  172.7 1456.2 %all-reduce.4.cloned.1.call-start = ((), (), s32[]{:S(2)}) async-start(), calls=%async_computation.2 | async-start | bytes 262144 | tf_op jit(solution)/shard_map/psum | solution.py:68
Sparse Core Ops, SparseCore 0:
  10.5 147.7 all-gather.2
  172.8 24.5 reduce-scatter.2
  1188.5 440.4 all-reduce.3
where the time goes:
time: 1640 us
  blocking collectives  994 us (61%)
  waiting for transfers between devices  603 us (37%)
    unnamed x2, blocking collectives  494 us
    psum x1, waiting for transfers between devices, on_device(): summed_docs = lax.psum(partial_docs, ('vocab', 'tok'))  440 us
    pmax x1, blocking collectives, gradient(): row_top = lax.pmax(local_top, 'vocab')  250 us
    psum x1, blocking collectives, gradient(): row_sum = lax.psum(jnp.sum(exponent, axis=1), 'vocab')  250 us
    all_gather x1, waiting for transfers between devices, on_device(): lax.all_gather(hidden, 'vocab', axis=0, tiled=True)  151 us
  transfers between devices with their start and end apart: 3, of which 3 were waited for; matrix products, arithmetic and copies ran while one was open for 0% of the time, Pallas kernels for 0%

commit v1 on v0

v1 whole, which is shorter than its diff:
```python
import functools

import jax
import jax.numpy as jnp
from jax import lax
from jax.experimental import pallas as pl
from jax.experimental.pallas import tpu as pltpu
from jax.sharding import Mesh
from jax.sharding import PartitionSpec as P

NY, NZ, NC, NX = 4, 16, 2, 4
SKETCH = 64
DOCS = 8
LANES = 128
F32 = jnp.float32
HIGHEST = lax.Precision.HIGHEST


def iota(shape, dim):
    return lax.broadcasted_iota(jnp.int32, shape, dim)


def softmax_kernel(place, targets, slab, own, other, out):
    core, x, first_col = place[0], place[1], place[2]
    mine = own[0, :64] + own[1, :64] + own[2, :64] + own[3, :64]
    theirs = other[0] + other[1] + other[2] + other[3]
    logits = jnp.concatenate(
        [jnp.where(core == 0, mine, theirs), jnp.where(core == 0, theirs, mine)], axis=0
    )
    rows, cols = logits.shape
    lane16 = iota((NZ, LANES), 1)
    row16 = iota((NZ, LANES), 0)
    pieces = []
    for c in range(NC):
        for y in range(NY):
            hit = lane16 == row16 * (NC * NX) + (c * NX + x)
            pieces.append(jnp.sum(jnp.where(hit, targets[y : y + 1, :], 0), axis=1, keepdims=True))
    target = jnp.concatenate(pieces, axis=0)
    is_target = iota((rows, cols), 1) + first_col == target
    top = jnp.max(logits, axis=1, keepdims=True)
    exponent = jnp.exp(logits - top)
    total = jnp.sum(exponent, axis=1, keepdims=True)
    target_logit = jnp.sum(jnp.where(is_target, logits, 0.0), axis=1, keepdims=True)
    rest = jnp.where(is_target, 0.0, exponent)
    high = rest.astype(jnp.bfloat16)
    low = (rest - high.astype(F32)).astype(jnp.bfloat16)
    slab_block = slab[...]
    grad = jnp.dot(high, slab_block, preferred_element_type=F32) + jnp.dot(
        low, slab_block, preferred_element_type=F32
    )
    at_target = jnp.dot(is_target.astype(jnp.bfloat16), slab_block, preferred_element_type=F32)
    both = jnp.concatenate([grad, at_target], axis=1)
    diagonal = iota((rows, LANES), 0) == iota((rows, LANES), 1)

    def as_row(column):
        return jnp.sum(jnp.where(diagonal, column, 0.0), axis=0, keepdims=True)

    feat = own[0, 64:65, :LANES] + own[1, 64:65, :LANES] + own[2, 64:65, :LANES] + own[3, 64:65, :LANES]
    zero = jnp.zeros((1, LANES), F32)
    stats = jnp.concatenate(
        [as_row(top), as_row(total), as_row(target_logit), zero, feat, zero, zero, zero], axis=0
    )
    for c in range(NC):
        for y in range(NY):
            first = (c * NY + y) * NZ
            out[y * NC + c, :NZ, :] = both[first : first + NZ]
            out[y * NC + c, NZ:, :] = stats


def merged(parts, count, core, y):
    stats = [parts[i, NZ:, :] for i in range(count)]
    top = functools.reduce(jnp.maximum, [s[0:1] for s in stats])
    scales = [jnp.exp(s[0:1] - top) for s in stats]
    total = sum(scale * s[1:2] for scale, s in zip(scales, stats))
    target_logit = sum(s[2:3] for s in stats)
    lane = iota((NZ, LANES), 1)
    mine = lane == iota((NZ, LANES), 0) + (core * NY + y) * NZ

    def as_column(row):
        return jnp.sum(jnp.where(mine, row, 0.0), axis=1, keepdims=True)

    left = lane < SKETCH
    both = sum(
        parts[i, :NZ, :] * jnp.where(left, as_column(scales[i]), 1.0) for i in range(count)
    )
    return both, top, total, target_logit, as_column


def merge_kernel(place, parts, out):
    core, y = place[0], place[3]
    both, top, total, target_logit, _ = merged(parts, NY * NC, core, y)
    feat = parts[y * NC + core, NZ + 4 : NZ + 5, :]
    zero = jnp.zeros((1, LANES), F32)
    out[:NZ, :] = both
    out[NZ:, :] = jnp.concatenate(
        [top, total, target_logit, zero, feat, zero, zero, zero], axis=0
    )


def finish_kernel(place, parts, out):
    core, y = place[0], place[3]
    both, top, total, target_logit, as_column = merged(parts, NZ, core, y)
    chance = jnp.exp(target_logit - top) / total
    weight = as_column((chance - 1.0).astype(jnp.bfloat16).astype(F32))
    grad = both / as_column(total) + weight * pltpu.roll(both, SKETCH, 1)
    row = iota((NZ, LANES), 0)
    feat = sum(jnp.where(row == z, parts[z, NZ + 4 : NZ + 5, :], 0.0) for z in range(NZ))
    out[...] = jnp.where(iota((NZ, LANES), 1) < SKETCH, grad, pltpu.roll(feat, SKETCH, 1))


def document_kernel(segments, rows, out):
    tokens, half = rows.shape[0], SKETCH * DOCS // 2
    values = rows[...]
    index = iota((tokens, half), 0)
    y, c, x, z = index // 128, (index // 64) % 2, (index // 16) % 4, index % 16
    token = y * 128 + z * 8 + c * 4 + x
    segment = segments[...]
    doc = iota((1, half), 1) % DOCS
    start = jnp.zeros((1, half), jnp.int32)
    stop = jnp.zeros((1, half), jnp.int32)
    inverse = jnp.zeros((DOCS, LANES), F32)
    below = jnp.zeros((1, 1), jnp.int32)
    for s in range(DOCS):
        here = jnp.sum(
            jnp.sum((segment == s).astype(jnp.int32), axis=1, keepdims=True), axis=0, keepdims=True
        )
        start = jnp.where(doc == s, below, start)
        below = below + here
        stop = jnp.where(doc == s, below, stop)
        inverse = jnp.where(iota((DOCS, LANES), 0) == s, 1.0 / jnp.sqrt(here.astype(F32)), inverse)
    member = (token >= start) & (token < stop)
    lane = iota((tokens, LANES), 1)
    swapped = pltpu.roll(values, SKETCH, 1)
    total = jnp.zeros((half, LANES), F32)
    for odd in range(2):
        pick = (iota((LANES, half), 0) == 2 * (iota((LANES, half), 1) // DOCS) + odd).astype(F32)
        spread = jnp.dot(values, pick, precision=HIGHEST, preferred_element_type=F32)
        spread = jnp.where(member, spread, 0.0)
        feat = jnp.where(lane < SKETCH, 0.0, values) if odd else jnp.where(lane < SKETCH, swapped, 0.0)
        total = total + lax.dot_general(
            spread, feat, (((0,), (0,)), ((), ())), precision=HIGHEST, preferred_element_type=F32
        )
    for pair in range(SKETCH // 2):
        out[:, pair * LANES : (pair + 1) * LANES] = total[pair * DOCS : (pair + 1) * DOCS] * inverse


def call(kernel, shape, *args):
    vmem = pl.BlockSpec(memory_space=pltpu.VMEM)
    smem = pl.BlockSpec(memory_space=pltpu.SMEM)
    return pl.pallas_call(
        kernel,
        out_shape=jax.ShapeDtypeStruct(shape, F32),
        in_specs=[smem if a.ndim == 1 else vmem for a in args],
        out_specs=vmem,
        compiler_params=pltpu.CompilerParams(vmem_limit_bytes=48 * 1024 * 1024),
    )(*args)


def to_all(block, axes, count):
    copies = jnp.broadcast_to(block[None], (count,) + block.shape)
    return lax.all_to_all(copies, axes, 0, 0, tiled=True)


def on_device(hidden, head, targets, segment_ids, grad_slab, feature_slab):
    y, c, x = lax.axis_index("y"), lax.axis_index("c"), lax.axis_index("x")
    z = lax.axis_index("z")
    width = hidden.shape[1]
    cols = head.shape[1]
    place = jnp.stack([c, x, ((y * NZ + z) * NC + c) * cols, y]).astype(jnp.int32)
    column = to_all(hidden, "z", NZ)
    column = column.transpose(1, 0, 2).reshape(NX * NZ, width)
    own = to_all(column, "y", NY).reshape(NY * NX * NZ, width)
    other = lax.ppermute(own, "c", [(0, 1), (1, 0)])
    own_logits = jnp.dot(own, head, preferred_element_type=F32)
    quarter = jnp.dot(hidden, feature_slab, preferred_element_type=F32)
    other_logits = jnp.dot(other, head, preferred_element_type=F32)

    def by_owner(a):
        return a.reshape(NY, NX, NZ, cols).transpose(1, 0, 2, 3).reshape(NX, NY * NZ, cols)

    feat = jnp.pad(quarter[:, None, :], ((0, 0), (0, 7), (0, cols - SKETCH)))
    outgoing = jnp.concatenate([by_owner(own_logits), feat, by_owner(other_logits)], axis=1)
    parts = lax.all_to_all(outgoing, "x", 0, 0, tiled=True)
    chunks = call(
        softmax_kernel,
        (NY * NC, NZ + 8, LANES),
        place,
        targets.reshape(NY, LANES),
        grad_slab,
        parts[:, :72],
        parts[:, 72:],
    )
    chunks = lax.all_to_all(chunks, ("y", "c"), 0, 0, tiled=True)
    merged_chunk = call(merge_kernel, (NZ + 8, LANES), place, chunks)
    rows = call(finish_kernel, (NZ, LANES), place, to_all(merged_chunk, "z", NZ))
    everyone = to_all(rows, ("y", "c", "x"), NY * NC * NX).reshape(-1, LANES)
    return call(
        document_kernel,
        (DOCS, SKETCH * SKETCH),
        segment_ids.reshape(NY, LANES),
        everyone,
    )


def solution(mesh):
    fine = Mesh(mesh.devices.reshape(NY, NZ, NC, NX), ("y", "z", "c", "x"))
    vocab = ("y", "z", "c")
    return jax.shard_map(
        on_device,
        mesh=fine,
        in_specs=(P(vocab, "x"), P("x", vocab), P(), P(), P(vocab, None), P("x", None)),
        out_specs=P(),
        check_vma=False,
    )
```

time: 1640 us -> 157 us (0.10)
  blocking collectives: 994 us -> 112 us
  waiting for transfers between devices: 603 us -> 17.2 us
    unnamed x2 -> x0, blocking collectives: 494 us -> none
    psum x1 -> x0, waiting for transfers between devices: 440 us -> none  [on_device(): summed_docs = lax.psum(partial_docs, ('vocab', 'tok'))]
    pmax x1 -> x0, blocking collectives: 250 us -> none  [gradient(): row_top = lax.pmax(local_top, 'vocab')]
    psum x1 -> x0, blocking collectives: 250 us -> none  [gradient(): row_sum = lax.psum(jnp.sum(exponent, axis=1), 'vocab')]
    all_gather x1 -> x0, waiting for transfers between devices: 151 us -> none  [on_device(): lax.all_gather(hidden, 'vocab', axis=0, tiled=True)]
    all_to_all x0 -> x5, blocking collectives: none -> 112 us  [the longest x4 103 us: to_all(): return lax.all_to_all(copies, axes, 0, 0, tiled=True)]
  transfers between devices with their start and end apart: 3 -> 2, of which waited for: 3 -> 2; matrix products, arithmetic and copies ran while one was open for 0% -> 1% of each run, Pallas kernels for 0% -> 0%
where the time goes in v1:
time: 157 us; the launch traced here: 156 us
  blocking collectives  112 us (71%)
  waiting for transfers between devices  17.2 us (11%)
  starting transfers between devices  14.5 us (9%)
  Pallas kernels  6.69 us (4%)
  matrix products  2.78 us (2%)
  local copies, waits for them, and re-layouts  1.9 us (1%)
    all_to_all x4, blocking collectives, to_all(): return lax.all_to_all(copies, axes, 0, 0, tiled=True)  103 us
    all_to_all x1, waiting for transfers between devices, on_device(): parts = lax.all_to_all(outgoing, 'x', 0, 0, tiled=True)  15 us
    ppermute x1, starting transfers between devices, on_device(): other = lax.ppermute(own, 'c', [(0, 1), (1, 0)])  10.3 us
    all_to_all x1, blocking collectives, on_device(): chunks = lax.all_to_all(chunks, ('y', 'c'), 0, 0, tiled=True)  8.87 us
    pallas_call x4, Pallas kernels, call(): pl.pallas_call(kernel, out_shape=jax.ShapeDtypeStruct(shape, F32), in_spe...  6.69 us
    all_to_all x1, starting transfers between devices, on_device(): parts = lax.all_to_all(outgoing, 'x', 0, 0, tiled=True)  4.15 us
  transfers between devices with their start and end apart: 2, of which 2 were waited for; matrix products, arithmetic and copies ran while one was open for 1% of the time, Pallas kernels for 0%

profile of v1, /device:TPU:1, one launch (start us, length us, event | category | flops | bytes accessed | tf_op | source)
XLA Modules:
  0.0 156.4 jit_solution(1937440415272077948)
XLA Ops:
  0.0 0.0 copy-start
  0.0 1.0 broadcast_in_dim.12
  1.0 38.4 %all_to_all.30 = bf16[16,4,4096]{2,1,0:T(4,128)(2,1)S(1)} all-to-all(bf16[16,4,4096]{2,1,0:T(4,128)(2,1)S(1)} %broadcast_in_dim.12), channel_id=1, replica_groups=mesh['y'=4,'z'=16,'c'=2,'x'=4] {'z'}, dimensions={0} | all-to-all | bytes 1048576 | tf_op jit(solution)/shard_map/all_to_all | solution.py:161
  39.4 0.3 copy.13
  39.7 0.2 broadcast_in_dim.14
  39.9 0.0 copy-start.3
  40.0 0.0 copy-start.5
  40.0 23.1 %all_to_all.31 = bf16[4,64,4096]{2,1,0:T(8,128)(2,1)S(1)} all-to-all(bf16[4,64,4096]{2,1,0:T(8,128)(2,1)S(1)} %broadcast_in_dim.14), channel_id=1, replica_groups=mesh['y'=4,'z'=16,'c'=2,'x'=4] {'y'}, dimensions={0} | all-to-all | bytes 4194304 | tf_op jit(solution)/shard_map/all_to_all | solution.py:161
  63.1 10.3 %collective-permute-start = (bf16[256,4096]{1,0:T(8,128)(2,1)S(1)}, bf16[256,4096]{1,0:T(8,128)(2,1)S(1)}, u32[]{:S(2)}, u32[]{:S(2)}) collective-permute-start(bf16[256,4096]{1,0:T(8,128)(2,1)S(1)} %bitcast.38), channel_id=1, source_target_pairs={{0,4},{4,0},{1,5},{5,1},{2,6},{6,2},{3,7},{7,3},{8,12},{12,8},{9,1... | collective-permute-start | bytes 6291464 | tf_op jit(solution)/shard_map/ppermute | solution.py:173
  73.4 0.0 copy-done
  73.4 0.0 copy-done.3
  73.4 0.2 fusion.7
  73.7 0.0 copy-done.5
  73.7 1.3 fusion.2
  75.0 2.2 %collective-permute-done = bf16[256,4096]{1,0:T(8,128)(2,1)S(1)} collective-permute-done((bf16[256,4096]{1,0:T(8,128)(2,1)S(1)}, bf16[256,4096]{1,0:T(8,128)(2,1)S(1)}, u32[]{:S(2)}, u32[]{:S(2)}) %collective-permute-start) | collective-permute-done | bytes 2097184 | tf_op jit(solution)/shard_map/ppermute | solution.py:173
  77.2 1.3 fusion.8
  78.5 0.0 copy-start.4
  78.5 1.1 fusion.5
  79.6 0.0 copy-start.1
  79.7 4.2 %all-to-all-start.2 = ((f32[4,136,512]{2,1,0:T(8,128)}), f32[4,136,512]{2,1,0:T(8,128)S(1)}, u32[]{:S(2)}, u32[]{:S(2)}) async-start(f32[4,136,512]{2,1,0:T(8,128)} %fusion.5), calls=%async_computation.2 | async-start | bytes 2228224 | tf_op jit(solution)/shard_map/all_to_all | solution.py:183
  83.8 0.0 copy-done.4
  83.8 0.1 copy.16.slab
  83.9 0.1 pad_add_fusion.place
  84.0 15.0 %all-to-all-done.2 = f32[4,136,512]{2,1,0:T(8,128)S(1)} async-done(((f32[4,136,512]{2,1,0:T(8,128)}), f32[4,136,512]{2,1,0:T(8,128)S(1)}, u32[]{:S(2)}, u32[]{:S(2)}) %all-to-all-start.2) | async-done | bytes 1114144 | tf_op jit(solution)/shard_map/all_to_all | solution.py:183
  99.1 0.0 copy-start.2
  99.1 0.0 copy-done.1
  99.1 1.1 shard_map.64
  100.3 8.9 %all_to_all.32.parts = f32[8,24,128]{2,1,0:T(8,128)S(1)} all-to-all(f32[8,24,128]{2,1,0:T(8,128)S(1)} %shard_map.64), channel_id=1, replica_groups=mesh['y'=4,'z'=16,'c'=2,'x'=4] {'y','c'}, dimensions={0} | all-to-all | bytes 196608 | tf_op jit(solution)/shard_map/all_to_all | solution.py:193
  109.1 0.6 shard_map.65
  109.8 24.8 %all_to_all.33.parts = f32[16,24,128]{2,1,0:T(8,128)S(1)} all-to-all(f32[16,24,128]{2,1,0:T(8,128)S(1)} %broadcast_in_dim.32), channel_id=1, replica_groups=mesh['y'=4,'z'=16,'c'=2,'x'=4] {'z'}, dimensions={0} | all-to-all | bytes 393216 | tf_op jit(solution)/shard_map/all_to_all | solution.py:161
  134.6 0.7 shard_map.66
  135.3 16.9 %all_to_all.34 = f32[32,16,128]{2,1,0:T(8,128)S(1)} all-to-all(f32[32,16,128]{2,1,0:T(8,128)S(1)} %broadcast_in_dim.33), channel_id=1, replica_groups=mesh['y'=4,'z'=16,'c'=2,'x'=4] {'y','c','x'}, dimensions={0} | all-to-all | bytes 524288 | tf_op jit(solution)/shard_map/all_to_all | solution.py:161
  152.2 0.0 copy-done.2
  152.2 4.2 %shard_map.67 = f32[8,4096]{1,0:T(8,128)} custom-call(s32[4,128]{1,0:T(4,128)S(1)} %bitcast.34, f32[512,128]{1,0:T(8,128)S(1)} %bitcast.32), custom_call_target="tpu_custom_call" | custom-call | tf_op jit(solution)/shard_map/pallas_call | solution.py:150
  (6 shorter events, 0.2 us)
Async XLA Ops:
  0.0 73.4 %copy-start = (bf16[4096,64]{0,1:T(8,128)(2,1)S(1)}, bf16[4096,64]{0,1:T(8,128)(2,1)}, u32[]{:S(2)}) copy-start(bf16[4096,64]{0,1:T(8,128)(2,1)} %param.11) | copy-start | bytes 1572868
  39.9 33.5 %copy-start.3 = (bf16[4,4096]{1,0:T(4,128)(2,1)S(1)}, bf16[4,4096]{1,0:T(4,128)(2,1)}, u32[]{:S(2)}) copy-start(bf16[4,4096]{1,0:T(4,128)(2,1)} %param.6) | copy-start | bytes 98308
  40.0 33.7 %copy-start.5 = (bf16[4096,512]{1,0:T(8,128)(2,1)S(1)}, bf16[4096,512]{1,0:T(8,128)(2,1)}, u32[]{:S(2)}) copy-start(bf16[4096,512]{1,0:T(8,128)(2,1)} %param.7) | copy-start | bytes 12582916
  63.1 14.1 %collective-permute-start = (bf16[256,4096]{1,0:T(8,128)(2,1)S(1)}, bf16[256,4096]{1,0:T(8,128)(2,1)S(1)}, u32[]{:S(2)}, u32[]{:S(2)}) collective-permute-start(bf16[256,4096]{1,0:T(8,128)(2,1)S(1)} %bitcast.38), channel_id=1, source_target_pairs={{0,4},{4,0},{1,5},{5,1},{2,6},{6,2},{3,7},{7,3},{8,12},{12,8},{9,1... | collective-permute-start | bytes 6291464 | tf_op jit(solution)/shard_map/ppermute | solution.py:173
  78.5 5.3 %copy-start.4 = (bf16[512,64]{0,1:T(8,128)(2,1)S(1)}, bf16[512,64]{0,1:T(8,128)(2,1)}, u32[]{:S(2)}) copy-start(bf16[512,64]{0,1:T(8,128)(2,1)} %param.10) | copy-start | bytes 196612
  79.6 19.5 %copy-start.1 = (s32[512]{0:T(512)S(1)}, s32[512]{0:T(512)}, u32[]{:S(2)}) copy-start(s32[512]{0:T(512)} %param.8) | copy-start | bytes 6148
  79.7 19.4 %all-to-all-start.2 = ((f32[4,136,512]{2,1,0:T(8,128)}), f32[4,136,512]{2,1,0:T(8,128)S(1)}, u32[]{:S(2)}, u32[]{:S(2)}) async-start(f32[4,136,512]{2,1,0:T(8,128)} %fusion.5), calls=%async_computation.2 | async-start | bytes 2228224 | tf_op jit(solution)/shard_map/all_to_all | solution.py:183
  99.1 53.2 %copy-start.2 = (s32[512]{0:T(512)S(1)}, s32[512]{0:T(512)}, u32[]{:S(2)}) copy-start(s32[512]{0:T(512)} %param.9) | copy-start | bytes 6148

commit v2 on v1

--- a/solution.py
+++ b/solution.py
@@ -28,6 +28,9 @@
         [jnp.where(core == 0, mine, theirs), jnp.where(core == 0, theirs, mine)], axis=0
     )
     rows, cols = logits.shape
+    top = jnp.max(logits, axis=1, keepdims=True)
+    exponent = jnp.exp(logits - top)
+    total = jnp.sum(exponent, axis=1, keepdims=True)
     lane16 = iota((NZ, LANES), 1)
     row16 = iota((NZ, LANES), 0)
     pieces = []
@@ -37,18 +40,17 @@
             pieces.append(jnp.sum(jnp.where(hit, targets[y : y + 1, :], 0), axis=1, keepdims=True))
     target = jnp.concatenate(pieces, axis=0)
     is_target = iota((rows, cols), 1) + first_col == target
-    top = jnp.max(logits, axis=1, keepdims=True)
-    exponent = jnp.exp(logits - top)
-    total = jnp.sum(exponent, axis=1, keepdims=True)
     target_logit = jnp.sum(jnp.where(is_target, logits, 0.0), axis=1, keepdims=True)
     rest = jnp.where(is_target, 0.0, exponent)
     high = rest.astype(jnp.bfloat16)
     low = (rest - high.astype(F32)).astype(jnp.bfloat16)
     slab_block = slab[...]
-    grad = jnp.dot(high, slab_block, preferred_element_type=F32) + jnp.dot(
-        low, slab_block, preferred_element_type=F32
-    )
-    at_target = jnp.dot(is_target.astype(jnp.bfloat16), slab_block, preferred_element_type=F32)
+
+    def sketched(a):
+        return lax.dot_general(a, slab_block, (((1,), (1,)), ((), ())), preferred_element_type=F32)
+
+    grad = sketched(high) + sketched(low)
+    at_target = sketched(is_target.astype(jnp.bfloat16))
     both = jnp.concatenate([grad, at_target], axis=1)
     diagonal = iota((rows, LANES), 0) == iota((rows, LANES), 1)
 
@@ -108,16 +110,21 @@
     out[...] = jnp.where(iota((NZ, LANES), 1) < SKETCH, grad, pltpu.roll(feat, SKETCH, 1))
 
 
+def halves(a):
+    high = a.astype(jnp.bfloat16)
+    return high, (a - high.astype(F32)).astype(jnp.bfloat16)
+
+
 def document_kernel(segments, rows, out):
     tokens, half = rows.shape[0], SKETCH * DOCS // 2
     values = rows[...]
-    index = iota((tokens, half), 0)
+    index = iota((1, tokens), 1)
     y, c, x, z = index // 128, (index // 64) % 2, (index // 16) % 4, index % 16
     token = y * 128 + z * 8 + c * 4 + x
     segment = segments[...]
-    doc = iota((1, half), 1) % DOCS
-    start = jnp.zeros((1, half), jnp.int32)
-    stop = jnp.zeros((1, half), jnp.int32)
+    doc = iota((half, 1), 0) % DOCS
+    start = jnp.zeros((half, 1), jnp.int32)
+    stop = jnp.zeros((half, 1), jnp.int32)
     inverse = jnp.zeros((DOCS, LANES), F32)
     below = jnp.zeros((1, 1), jnp.int32)
     for s in range(DOCS):
@@ -129,17 +136,21 @@
         stop = jnp.where(doc == s, below, stop)
         inverse = jnp.where(iota((DOCS, LANES), 0) == s, 1.0 / jnp.sqrt(here.astype(F32)), inverse)
     member = (token >= start) & (token < stop)
-    lane = iota((tokens, LANES), 1)
+    left = iota((tokens, LANES), 1) < SKETCH
     swapped = pltpu.roll(values, SKETCH, 1)
+    grad = halves(values)
     total = jnp.zeros((half, LANES), F32)
     for odd in range(2):
-        pick = (iota((LANES, half), 0) == 2 * (iota((LANES, half), 1) // DOCS) + odd).astype(F32)
-        spread = jnp.dot(values, pick, precision=HIGHEST, preferred_element_type=F32)
-        spread = jnp.where(member, spread, 0.0)
-        feat = jnp.where(lane < SKETCH, 0.0, values) if odd else jnp.where(lane < SKETCH, swapped, 0.0)
-        total = total + lax.dot_general(
-            spread, feat, (((0,), (0,)), ((), ())), precision=HIGHEST, preferred_element_type=F32
-        )
+        pick = iota((half, LANES), 1) == 2 * (iota((half, LANES), 0) // DOCS) + odd
+        pick = pick.astype(F32).astype(jnp.bfloat16)
+        spread = [
+            lax.dot_general(pick, g, (((1,), (1,)), ((), ())), preferred_element_type=F32)
+            for g in grad
+        ]
+        high, low = [jnp.where(member, a, 0.0).astype(jnp.bfloat16) for a in spread]
+        feat_high, feat_low = halves(jnp.where(left, 0.0, values) if odd else jnp.where(left, swapped, 0.0))
+        for a, b in ((high, feat_high), (high, feat_low), (low, feat_high)):
+            total = total + jnp.dot(a, b, preferred_element_type=F32)
     for pair in range(SKETCH // 2):
         out[:, pair * LANES : (pair + 1) * LANES] = total[pair * DOCS : (pair + 1) * DOCS] * inverse
 
@@ -167,7 +178,8 @@
     width = hidden.shape[1]
     cols = head.shape[1]
     place = jnp.stack([c, x, ((y * NZ + z) * NC + c) * cols, y]).astype(jnp.int32)
-    column = to_all(hidden, "z", NZ)
+    hidden, place = lax.optimization_barrier((hidden, place))
+    column = lax.all_gather(hidden, "z")
     column = column.transpose(1, 0, 2).reshape(NX * NZ, width)
     own = to_all(column, "y", NY).reshape(NY * NX * NZ, width)
     other = lax.ppermute(own, "c", [(0, 1), (1, 0)])
@@ -186,7 +198,7 @@
         (NY * NC, NZ + 8, LANES),
         place,
         targets.reshape(NY, LANES),
-        grad_slab,
+        grad_slab.T,
         parts[:, :72],
         parts[:, 72:],
     )

time: 157 us -> 140 us (0.89)
  waiting for transfers between devices: 17.2 us -> 2.19 us
  blocking collectives: 112 us -> 118 us
  starting transfers between devices: 14.5 us -> 11.5 us
  Pallas kernels: 6.69 us -> 4.18 us
    all_to_all x4 -> x3, blocking collectives: 103 us -> 58 us  [to_all(): return lax.all_to_all(copies, axes, 0, 0, tiled=True)]
    all_gather x0 -> x1, blocking collectives: none -> 32.2 us  [on_device(): column = lax.all_gather(hidden, 'z')]
    all_to_all x0 -> x1, blocking collectives: none -> 19.2 us  [on_device(): parts = lax.all_to_all(outgoing, 'x', 0, 0, tiled=True)]
    all_to_all x1 -> x0, waiting for transfers between devices: 15 us -> none  [on_device(): parts = lax.all_to_all(outgoing, 'x', 0, 0, tiled=True)]
    all_to_all x1 -> x0, starting transfers between devices: 4.15 us -> none  [on_device(): parts = lax.all_to_all(outgoing, 'x', 0, 0, tiled=True)]
    pallas_call x4, Pallas kernels: 6.69 us -> 4.18 us  [call(): pl.pallas_call(kernel, out_shape=jax.ShapeDtypeStruct(shape, F32), in_spe...]
  transfers between devices with their start and end apart: 2 -> 1, of which waited for: 2 -> 1; matrix products, arithmetic and copies ran while one was open for 1% -> 1% of each run, Pallas kernels for 0% -> 0%
where the time goes in v2:
time: 140 us
  blocking collectives  118 us (84%)
  starting transfers between devices  11.5 us (8%)
  Pallas kernels  4.18 us (3%)
  matrix products  2.73 us (2%)
  waiting for transfers between devices  2.19 us (2%)
    all_to_all x3, blocking collectives, to_all(): return lax.all_to_all(copies, axes, 0, 0, tiled=True)  58 us
    all_gather x1, blocking collectives, on_device(): column = lax.all_gather(hidden, 'z')  32.2 us
    all_to_all x1, blocking collectives, on_device(): parts = lax.all_to_all(outgoing, 'x', 0, 0, tiled=True)  19.2 us
    ppermute x1, starting transfers between devices, on_device(): other = lax.ppermute(own, 'c', [(0, 1), (1, 0)])  11.5 us
    all_to_all x1, blocking collectives, on_device(): chunks = lax.all_to_all(chunks, ('y', 'c'), 0, 0, tiled=True)  8.88 us
    pallas_call x4, Pallas kernels, call(): pl.pallas_call(kernel, out_shape=jax.ShapeDtypeStruct(shape, F32), in_spe...  4.18 us
  transfers between devices with their start and end apart: 1, of which 1 were waited for; matrix products, arithmetic and copies ran while one was open for 1% of the time, Pallas kernels for 0%

profile of v2, /device:TPU:1, one launch (start us, length us, event | category | flops | bytes accessed | tf_op | source)
XLA Modules:
  0.0 139.9 jit_solution(15580923413887839809)
XLA Ops:
  0.0 0.0 copy-start
  0.0 0.1 pad_add_fusion.place
  0.1 32.2 %all-gather.1 = bf16[16,4,4096]{2,1,0:T(4,128)(2,1)S(1)} all-gather(bf16[1,4,4096]{2,1,0:T(4,128)(2,1)} %bitcast.44), channel_id=2, replica_groups=mesh['y'=4,'z'=16,'c'=2,'x'=4] {'z'}, dimensions={0}, use_global_device_ids=true | all-gather | bytes 557056 | tf_op jit(solution)/shard_map/all_gather | solution.py:182
  32.3 0.3 copy.14
  32.6 0.2 broadcast_in_dim.11
  32.8 0.0 copy-start.4
  32.8 0.0 copy-start.5
  32.8 21.9 %all_to_all.25 = bf16[4,64,4096]{2,1,0:T(8,128)(2,1)S(1)} all-to-all(bf16[4,64,4096]{2,1,0:T(8,128)(2,1)S(1)} %broadcast_in_dim.11), channel_id=1, replica_groups=mesh['y'=4,'z'=16,'c'=2,'x'=4] {'y'}, dimensions={0} | all-to-all | bytes 4194304 | tf_op jit(solution)/shard_map/all_to_all | solution.py:172
  54.8 11.5 %collective-permute-start = (bf16[256,4096]{1,0:T(8,128)(2,1)S(1)}, bf16[256,4096]{1,0:T(8,128)(2,1)S(1)}, u32[]{:S(2)}, u32[]{:S(2)}) collective-permute-start(bf16[256,4096]{1,0:T(8,128)(2,1)S(1)} %bitcast.41), channel_id=1, source_target_pairs={{0,4},{4,0},{1,5},{5,1},{2,6},{6,2},{3,7},{7,3},{8,12},{12,8},{9,1... | collective-permute-start | bytes 6291464 | tf_op jit(solution)/shard_map/ppermute | solution.py:185
  66.3 0.0 copy-done
  66.3 0.0 copy-done.4
  66.3 0.2 fusion.7
  66.5 0.0 copy-done.5
  66.5 1.3 fusion.2
  67.8 2.2 %collective-permute-done = bf16[256,4096]{1,0:T(8,128)(2,1)S(1)} collective-permute-done((bf16[256,4096]{1,0:T(8,128)(2,1)S(1)}, bf16[256,4096]{1,0:T(8,128)(2,1)S(1)}, u32[]{:S(2)}, u32[]{:S(2)}) %collective-permute-start) | collective-permute-done | bytes 2097184 | tf_op jit(solution)/shard_map/ppermute | solution.py:185
  70.0 1.2 fusion.8
  71.3 0.1 fusion.5
  71.4 0.0 copy-start.1
  71.4 0.0 copy-start.2
  71.5 19.2 %all_to_all.26 = f32[4,136,512]{2,1,0:T(8,128)S(1)} all-to-all(f32[4,136,512]{2,1,0:T(8,128)S(1)} %fusion.5), channel_id=1, replica_groups=mesh['y'=4,'z'=16,'c'=2,'x'=4] {'x'}, dimensions={0} | all-to-all | bytes 2228224 | tf_op jit(solution)/shard_map/all_to_all | solution.py:195
  90.7 0.0 copy-start.3
  90.7 0.0 copy-done.1
  90.7 0.0 copy-done.2
  90.8 1.1 shard_map.64
  91.9 8.9 %all_to_all.27.parts = f32[8,24,128]{2,1,0:T(8,128)S(1)} all-to-all(f32[8,24,128]{2,1,0:T(8,128)S(1)} %shard_map.64), channel_id=1, replica_groups=mesh['y'=4,'z'=16,'c'=2,'x'=4] {'y','c'}, dimensions={0} | all-to-all | bytes 196608 | tf_op jit(solution)/shard_map/all_to_all | solution.py:205
  100.7 0.6 shard_map.65
  101.4 19.2 %all_to_all.28.parts = f32[16,24,128]{2,1,0:T(8,128)S(1)} all-to-all(f32[16,24,128]{2,1,0:T(8,128)S(1)} %broadcast_in_dim.25), channel_id=1, replica_groups=mesh['y'=4,'z'=16,'c'=2,'x'=4] {'z'}, dimensions={0} | all-to-all | bytes 393216 | tf_op jit(solution)/shard_map/all_to_all | solution.py:172
  120.6 0.7 shard_map.66
  121.4 16.9 %all_to_all.29 = f32[32,16,128]{2,1,0:T(8,128)S(1)} all-to-all(f32[32,16,128]{2,1,0:T(8,128)S(1)} %broadcast_in_dim.26), channel_id=1, replica_groups=mesh['y'=4,'z'=16,'c'=2,'x'=4] {'y','c','x'}, dimensions={0} | all-to-all | bytes 524288 | tf_op jit(solution)/shard_map/all_to_all | solution.py:172
  138.3 0.0 copy-done.3
  138.3 1.7 %shard_map.67 = f32[8,4096]{1,0:T(8,128)} custom-call(s32[4,128]{1,0:T(4,128)S(1)} %bitcast.37, f32[512,128]{1,0:T(8,128)S(1)} %bitcast.34), custom_call_target="tpu_custom_call" | custom-call | tf_op jit(solution)/shard_map/pallas_call | solution.py:161
  (6 shorter events, 0.2 us)
Async XLA Ops:
  0.0 66.3 %copy-start = (bf16[4096,64]{0,1:T(8,128)(2,1)S(1)}, bf16[4096,64]{0,1:T(8,128)(2,1)}, u32[]{:S(2)}) copy-start(bf16[4096,64]{0,1:T(8,128)(2,1)} %param.11) | copy-start | bytes 1572868
  32.8 33.5 %copy-start.4 = (bf16[4,4096]{1,0:T(4,128)(2,1)S(1)}, bf16[4,4096]{1,0:T(4,128)(2,1)}, u32[]{:S(2)}) copy-start(bf16[4,4096]{1,0:T(4,128)(2,1)} %param.6) | copy-start | bytes 98308
  32.8 33.7 %copy-start.5 = (bf16[4096,512]{1,0:T(8,128)(2,1)S(1)}, bf16[4096,512]{1,0:T(8,128)(2,1)}, u32[]{:S(2)}) copy-start(bf16[4096,512]{1,0:T(8,128)(2,1)} %param.7) | copy-start | bytes 12582916
  54.8 15.3 %collective-permute-start = (bf16[256,4096]{1,0:T(8,128)(2,1)S(1)}, bf16[256,4096]{1,0:T(8,128)(2,1)S(1)}, u32[]{:S(2)}, u32[]{:S(2)}) collective-permute-start(bf16[256,4096]{1,0:T(8,128)(2,1)S(1)} %bitcast.41), channel_id=1, source_target_pairs={{0,4},{4,0},{1,5},{5,1},{2,6},{6,2},{3,7},{7,3},{8,12},{12,8},{9,1... | collective-permute-start | bytes 6291464 | tf_op jit(solution)/shard_map/ppermute | solution.py:185
  71.4 19.3 %copy-start.1 = (bf16[512,64]{0,1:T(8,128)(2,1)S(1)}, bf16[512,64]{0,1:T(8,128)(2,1)}, u32[]{:S(2)}) copy-start(bf16[512,64]{0,1:T(8,128)(2,1)} %param.10) | copy-start | bytes 196612
  71.4 19.3 %copy-start.2 = (s32[512]{0:T(512)S(1)}, s32[512]{0:T(512)}, u32[]{:S(2)}) copy-start(s32[512]{0:T(512)} %param.8) | copy-start | bytes 6148
  90.7 47.6 %copy-start.3 = (s32[512]{0:T(512)S(1)}, s32[512]{0:T(512)}, u32[]{:S(2)}) copy-start(s32[512]{0:T(512)} %param.9) | copy-start | bytes 6148

commit v3 on v2

--- a/solution.py
+++ b/solution.py
@@ -20,63 +20,58 @@
     return lax.broadcasted_iota(jnp.int32, shape, dim)
 
 
-def softmax_kernel(place, targets, slab, own, other, out):
-    core, x, first_col = place[0], place[1], place[2]
-    mine = own[0, :64] + own[1, :64] + own[2, :64] + own[3, :64]
-    theirs = other[0] + other[1] + other[2] + other[3]
-    logits = jnp.concatenate(
-        [jnp.where(core == 0, mine, theirs), jnp.where(core == 0, theirs, mine)], axis=0
-    )
-    rows, cols = logits.shape
-    top = jnp.max(logits, axis=1, keepdims=True)
-    exponent = jnp.exp(logits - top)
-    total = jnp.sum(exponent, axis=1, keepdims=True)
-    lane16 = iota((NZ, LANES), 1)
-    row16 = iota((NZ, LANES), 0)
-    pieces = []
-    for c in range(NC):
-        for y in range(NY):
-            hit = lane16 == row16 * (NC * NX) + (c * NX + x)
-            pieces.append(jnp.sum(jnp.where(hit, targets[y : y + 1, :], 0), axis=1, keepdims=True))
-    target = jnp.concatenate(pieces, axis=0)
-    is_target = iota((rows, cols), 1) + first_col == target
-    target_logit = jnp.sum(jnp.where(is_target, logits, 0.0), axis=1, keepdims=True)
-    rest = jnp.where(is_target, 0.0, exponent)
-    high = rest.astype(jnp.bfloat16)
-    low = (rest - high.astype(F32)).astype(jnp.bfloat16)
-    slab_block = slab[...]
-
-    def sketched(a):
-        return lax.dot_general(a, slab_block, (((1,), (1,)), ((), ())), preferred_element_type=F32)
-
-    grad = sketched(high) + sketched(low)
-    at_target = sketched(is_target.astype(jnp.bfloat16))
+def softmax_kernel(place, targets, slab, partner_slab, parts, out):
+    core, x, first_col, partner_col = place[0], place[1], place[2], place[4]
+    rows, cols = NY * NZ, slab.shape[1]
+    summed = parts[0, :rows] + parts[1, :rows] + parts[2, :rows] + parts[3, :rows]
+    blocks = [(summed[:, :cols], slab, first_col), (summed[:, cols:], partner_slab, partner_col)]
+    hit = iota((NZ, LANES), 1) == iota((NZ, LANES), 0) * (NC * NX) + (core * NX + x)
+    target = jnp.concatenate(
+        [
+            jnp.sum(jnp.where(hit, targets[y : y + 1, :], 0), axis=1, keepdims=True)
+            for y in range(NY)
+        ],
+        axis=0,
+    )
+    top = jnp.maximum(*[jnp.max(logits, axis=1, keepdims=True) for logits, _, _ in blocks])
+    total = target_logit = grad = at_target = 0.0
+    for logits, slab_ref, first in blocks:
+        is_target = iota((rows, cols), 1) + first == target
+        exponent = jnp.exp(logits - top)
+        total += jnp.sum(exponent, axis=1, keepdims=True)
+        target_logit += jnp.sum(jnp.where(is_target, logits, 0.0), axis=1, keepdims=True)
+        slab_block = slab_ref[...]
+
+        def sketched(a):
+            return lax.dot_general(a, slab_block, (((1,), (1,)), ((), ())), preferred_element_type=F32)
+
+        high, low = halves(jnp.where(is_target, 0.0, exponent))
+        grad += sketched(high) + sketched(low)
+        at_target += sketched(is_target.astype(jnp.bfloat16))
     both = jnp.concatenate([grad, at_target], axis=1)
     diagonal = iota((rows, LANES), 0) == iota((rows, LANES), 1)
 
     def as_row(column):
         return jnp.sum(jnp.where(diagonal, column, 0.0), axis=0, keepdims=True)
 
-    feat = own[0, 64:65, :LANES] + own[1, 64:65, :LANES] + own[2, 64:65, :LANES] + own[3, 64:65, :LANES]
+    feat = sum(parts[i, rows : rows + 1, :LANES] for i in range(NX))
     zero = jnp.zeros((1, LANES), F32)
     stats = jnp.concatenate(
         [as_row(top), as_row(total), as_row(target_logit), zero, feat, zero, zero, zero], axis=0
     )
-    for c in range(NC):
-        for y in range(NY):
-            first = (c * NY + y) * NZ
-            out[y * NC + c, :NZ, :] = both[first : first + NZ]
-            out[y * NC + c, NZ:, :] = stats
-
-
-def merged(parts, count, core, y):
+    for y in range(NY):
+        out[y, :NZ, :] = both[y * NZ : (y + 1) * NZ]
+        out[y, NZ:, :] = stats
+
+
+def merged(parts, count, y):
     stats = [parts[i, NZ:, :] for i in range(count)]
     top = functools.reduce(jnp.maximum, [s[0:1] for s in stats])
     scales = [jnp.exp(s[0:1] - top) for s in stats]
     total = sum(scale * s[1:2] for scale, s in zip(scales, stats))
     target_logit = sum(s[2:3] for s in stats)
     lane = iota((NZ, LANES), 1)
-    mine = lane == iota((NZ, LANES), 0) + (core * NY + y) * NZ
+    mine = lane == iota((NZ, LANES), 0) + y * NZ
 
     def as_column(row):
         return jnp.sum(jnp.where(mine, row, 0.0), axis=1, keepdims=True)
@@ -89,9 +84,9 @@
 
 
 def merge_kernel(place, parts, out):
-    core, y = place[0], place[3]
-    both, top, total, target_logit, _ = merged(parts, NY * NC, core, y)
-    feat = parts[y * NC + core, NZ + 4 : NZ + 5, :]
+    y = place[3]
+    both, top, total, target_logit, _ = merged(parts, NY, y)
+    feat = parts[y, NZ + 4 : NZ + 5, :]
     zero = jnp.zeros((1, LANES), F32)
     out[:NZ, :] = both
     out[NZ:, :] = jnp.concatenate(
@@ -100,9 +95,9 @@
 
 
 def finish_kernel(place, parts, out):
-    core, y = place[0], place[3]
-    both, top, total, target_logit, as_column = merged(parts, NZ, core, y)
-    chance = jnp.exp(target_logit - top) / total
+    y = place[3]
+    both, top, total, target_logit, as_column = merged(parts, NZ, y)
+    chance = jnp.exp(target_logit - top) / jnp.where(total > 0, total, 1.0)
     weight = as_column((chance - 1.0).astype(jnp.bfloat16).astype(F32))
     grad = both / as_column(total) + weight * pltpu.roll(both, SKETCH, 1)
     row = iota((NZ, LANES), 0)
@@ -155,6 +150,45 @@
         out[:, pair * LANES : (pair + 1) * LANES] = total[pair * DOCS : (pair + 1) * DOCS] * inverse
 
 
+def logits_kernel(rows, own, partner, hidden, feature_slab, out, weights, total, staged, sems, out_sems):
+    steps = sems.shape[0]
+    depth, cols = own.shape[0] // steps, own.shape[1]
+    copies = []
+    for k in range(steps):
+        part = pl.ds(k * depth, depth)
+        for side, head in enumerate((own, partner)):
+            target = weights.at[part, pl.ds(side * cols, cols)]
+            copies.append(pltpu.make_async_copy(head.at[part], target, sems.at[k, side]))
+    for copy in copies:
+        copy.start()
+    block = NY * NZ
+    quarter = lax.dot_general(
+        hidden[...], feature_slab[...], (((1,), (1,)), ((), ())), preferred_element_type=F32
+    )
+    feat = jnp.concatenate([quarter, jnp.zeros((NX, LANES - SKETCH), F32)], axis=1)
+    for j in range(NX):
+        staged[j, block:, :] = jnp.zeros((8, 2 * cols), F32)
+        staged[j, block : block + 1, :LANES] = feat[j : j + 1]
+    for k in range(steps):
+        copies[2 * k].wait()
+        copies[2 * k + 1].wait()
+        part = pl.ds(k * depth, depth)
+        term = jnp.dot(rows[:, part], weights[part, :], preferred_element_type=F32)
+        if k == 0:
+            total[...] = term
+        elif k < steps - 1:
+            total[...] += term
+    sends = []
+    for j in range(NX):
+        for y in range(NY):
+            first = (y * NX + j) * NZ
+            staged[j, y * NZ : (y + 1) * NZ, :] = total[first : first + NZ, :] + term[first : first + NZ]
+        sends.append(pltpu.make_async_copy(staged.at[j], out.at[j], out_sems.at[j]))
+        sends[j].start()
+    for send in sends:
+        send.wait()
+
+
 def call(kernel, shape, *args):
     vmem = pl.BlockSpec(memory_space=pltpu.VMEM)
     smem = pl.BlockSpec(memory_space=pltpu.SMEM)
@@ -163,8 +197,29 @@
         out_shape=jax.ShapeDtypeStruct(shape, F32),
         in_specs=[smem if a.ndim == 1 else vmem for a in args],
         out_specs=vmem,
-        compiler_params=pltpu.CompilerParams(vmem_limit_bytes=48 * 1024 * 1024),
+        compiler_params=pltpu.CompilerParams(vmem_limit_bytes=16 * 1024 * 1024),
     )(*args)
+
+
+def all_logits(rows, own, partner, hidden, feature_slab):
+    vmem = pl.BlockSpec(memory_space=pltpu.VMEM)
+    far = pl.BlockSpec(memory_space=pltpu.HBM)
+    width, cols = own.shape
+    shape = (NX, NY * NZ + 8, 2 * cols)
+    return pl.pallas_call(
+        logits_kernel,
+        out_shape=jax.ShapeDtypeStruct(shape, F32),
+        in_specs=[vmem, far, far, vmem, vmem],
+        out_specs=far,
+        scratch_shapes=[
+            pltpu.VMEM((width, 2 * cols), own.dtype),
+            pltpu.VMEM((rows.shape[0], 2 * cols), F32),
+            pltpu.VMEM(shape, F32),
+            pltpu.SemaphoreType.DMA((4, 2)),
+            pltpu.SemaphoreType.DMA((NX,)),
+        ],
+        compiler_params=pltpu.CompilerParams(vmem_limit_bytes=32 * 1024 * 1024),
+    )(rows, own, partner, hidden, feature_slab)
 
 
 def to_all(block, axes, count):
@@ -177,32 +232,28 @@
     z = lax.axis_index("z")
     width = hidden.shape[1]
     cols = head.shape[1]
-    place = jnp.stack([c, x, ((y * NZ + z) * NC + c) * cols, y]).astype(jnp.int32)
+    column_of = (y * NZ + z) * NC
+    place = jnp.stack([c, x, (column_of + c) * cols, y, (column_of + 1 - c) * cols]).astype(jnp.int32)
     hidden, place = lax.optimization_barrier((hidden, place))
+    swap = [(0, 1), (1, 0)]
+    partner_head = lax.ppermute(head, "c", swap)
+    partner_slab = lax.ppermute(grad_slab.T, "c", swap)
     column = lax.all_gather(hidden, "z")
     column = column.transpose(1, 0, 2).reshape(NX * NZ, width)
-    own = to_all(column, "y", NY).reshape(NY * NX * NZ, width)
-    other = lax.ppermute(own, "c", [(0, 1), (1, 0)])
-    own_logits = jnp.dot(own, head, preferred_element_type=F32)
-    quarter = jnp.dot(hidden, feature_slab, preferred_element_type=F32)
-    other_logits = jnp.dot(other, head, preferred_element_type=F32)
-
-    def by_owner(a):
-        return a.reshape(NY, NX, NZ, cols).transpose(1, 0, 2, 3).reshape(NX, NY * NZ, cols)
-
-    feat = jnp.pad(quarter[:, None, :], ((0, 0), (0, 7), (0, cols - SKETCH)))
-    outgoing = jnp.concatenate([by_owner(own_logits), feat, by_owner(other_logits)], axis=1)
+    rows = to_all(column, "y", NY).reshape(NY * NX * NZ, width)
+
+    outgoing = all_logits(rows, head, partner_head, hidden, feature_slab.T)
     parts = lax.all_to_all(outgoing, "x", 0, 0, tiled=True)
     chunks = call(
         softmax_kernel,
-        (NY * NC, NZ + 8, LANES),
+        (NY, NZ + 8, LANES),
         place,
         targets.reshape(NY, LANES),
         grad_slab.T,
-        parts[:, :72],
-        parts[:, 72:],
-    )
-    chunks = lax.all_to_all(chunks, ("y", "c"), 0, 0, tiled=True)
+        partner_slab,
+        parts,
+    )
+    chunks = lax.all_to_all(chunks, "y", 0, 0, tiled=True)
     merged_chunk = call(merge_kernel, (NZ + 8, LANES), place, chunks)
     rows = call(finish_kernel, (NZ, LANES), place, to_all(merged_chunk, "z", NZ))
     everyone = to_all(rows, ("y", "c", "x"), NY * NC * NX).reshape(-1, LANES)

time: 140 us -> 133 us (0.950)
  blocking collectives: 118 us -> 98 us
  starting transfers between devices: 11.5 us -> 23.6 us
  Pallas kernels: 4.18 us -> 9.24 us
  matrix products: 2.73 us -> 0 us
    all_to_all x2 -> x1, blocking collectives: 28.1 us -> 7.04 us  [on_device(): chunks = lax.all_to_all(chunks, 'y', 0, 0, tiled=True)]
    ppermute x1 -> x2, starting transfers between devices: 11.5 us -> 19.4 us  [the longest x1 10.7 us: on_device(): partner_slab = lax.ppermute(grad_slab.T, 'c', swap)]
    all_to_all x3, blocking collectives: 58 us -> 64.9 us  [to_all(): return lax.all_to_all(copies, axes, 0, 0, tiled=True)]
    all_gather x1, blocking collectives: 32.2 us -> 26.1 us  [on_device(): column = lax.all_gather(hidden, 'z')]
    pallas_call x0 -> x1, Pallas kernels: none -> 5.12 us  [all_logits(): pl.pallas_call(logits_kernel, out_shape=jax.ShapeDtypeStruct(shape, F32),...]
    all_to_all x0 -> x1, starting transfers between devices: none -> 4.16 us  [on_device(): parts = lax.all_to_all(outgoing, 'x', 0, 0, tiled=True)]
    dot_general x3 -> x0, matrix products: 2.73 us -> none  [the longest x1 1.25 us: on_device(): own_logits = jnp.dot(own, head, preferred_element_type=F32)]
  transfers between devices with their start and end apart: 1 -> 3, of which waited for: 1 -> 1; matrix products, arithmetic and copies ran while one was open for 1% -> 0% of each run, Pallas kernels for 0% -> 0%
where the time goes in v3:
time: 133 us
  blocking collectives  98 us (74%)
  starting transfers between devices  23.6 us (18%)
  Pallas kernels  9.24 us (7%)
    all_to_all x3, blocking collectives, to_all(): return lax.all_to_all(copies, axes, 0, 0, tiled=True)  64.9 us
    all_gather x1, blocking collectives, on_device(): column = lax.all_gather(hidden, 'z')  26.1 us
    ppermute x1, starting transfers between devices, on_device(): partner_slab = lax.ppermute(grad_slab.T, 'c', swap)  10.7 us
    ppermute x1, starting transfers between devices, on_device(): partner_head = lax.ppermute(head, 'c', swap)  8.78 us
    all_to_all x1, blocking collectives, on_device(): chunks = lax.all_to_all(chunks, 'y', 0, 0, tiled=True)  7.04 us
    pallas_call x1, Pallas kernels, all_logits(): pl.pallas_call(logits_kernel, out_shape=jax.ShapeDtypeStruct(shape, F32),...  5.12 us
    all_to_all x1, starting transfers between devices, on_device(): parts = lax.all_to_all(outgoing, 'x', 0, 0, tiled=True)  4.16 us
    pallas_call x4, Pallas kernels, call(): pl.pallas_call(kernel, out_shape=jax.ShapeDtypeStruct(shape, F32), in_spe...  4.12 us
  transfers between devices with their start and end apart: 3, of which 1 were waited for; matrix products, arithmetic and copies ran while one was open for 0% of the time, Pallas kernels for 0%

profile of v3, /device:TPU:1, one launch (start us, length us, event | category | flops | bytes accessed | tf_op | source)
XLA Modules:
  0.0 132.5 jit_solution(8604411132716100174)
XLA Ops:
  0.0 8.8 %collective-permute-start.1 = (bf16[4096,512]{1,0:T(8,128)(2,1)}, bf16[4096,512]{1,0:T(8,128)(2,1)}, u32[]{:S(2)}, u32[]{:S(2)}) collective-permute-start(bf16[4096,512]{1,0:T(8,128)(2,1)} %own.1), channel_id=1, source_target_pairs={{0,4},{4,0},{1,5},{5,1},{2,6},{6,2},{3,7},{7,3},{8,12},{12,8},{9,1... | collective-permute-start | bytes 12582920 | tf_op jit(solution)/shard_map/ppermute | solution.py:239
  8.8 0.1 stack.23.place
  8.9 26.1 %all-gather.1 = bf16[16,4,4096]{2,1,0:T(4,128)(2,1)S(1)} all-gather(bf16[1,4,4096]{2,1,0:T(4,128)(2,1)} %bitcast.18), channel_id=2, replica_groups=mesh['y'=4,'z'=16,'c'=2,'x'=4] {'z'}, dimensions={0}, use_global_device_ids=true | all-gather | bytes 557056 | tf_op jit(solution)/shard_map/all_gather | solution.py:241
  34.9 0.3 copy.8
  35.2 0.0 copy-start.1
  35.2 0.0 copy-start.2
  35.3 0.2 broadcast_in_dim.9
  35.5 0.0 copy-start
  35.5 23.2 %all_to_all.25 = bf16[4,64,4096]{2,1,0:T(8,128)(2,1)S(1)} all-to-all(bf16[4,64,4096]{2,1,0:T(8,128)(2,1)S(1)} %broadcast_in_dim.9), channel_id=1, replica_groups=mesh['y'=4,'z'=16,'c'=2,'x'=4] {'y'}, dimensions={0} | all-to-all | bytes 4194304 | tf_op jit(solution)/shard_map/all_to_all | solution.py:227
  58.7 0.0 collective-permute-done.1.partner
  58.7 0.0 copy-done.1
  58.7 0.0 copy-done.2
  58.7 0.0 copy-done
  58.7 5.1 %shard_map.64 = f32[4,72,1024]{2,1,0:T(8,128)} custom-call(bf16[256,4096]{1,0:T(8,128)(2,1)S(1)} %bitcast.15, bf16[4096,512]{1,0:T(8,128)(2,1)S(1)} %copy-done, bf16[4096,512]{1,0:T(8,128)(2,1)} %collective-permute-done.1.partner, bf16[4,4096]{1,0:T(4,128)(2,1)S(1)} %copy-done.2, bf16[64,4096]{1,0:T(8,128)(2,1)S(1)} %bitcast.17), custom_call_target="tpu_custom_call" | custom-call | tf_op jit(solution)/shard_map/pallas_call | solution.py:209
  63.9 0.0 copy-start.3
  63.9 0.0 copy-start.4
  63.9 4.2 %all-to-all-start.1 = ((f32[4,72,1024]{2,1,0:T(8,128)}), f32[4,72,1024]{2,1,0:T(8,128)S(1)}, u32[]{:S(2)}, u32[]{:S(2)}) async-start(f32[4,72,1024]{2,1,0:T(8,128)} %shard_map.64), calls=%async_computation.1 | async-start | bytes 2359296 | tf_op jit(solution)/shard_map/all_to_all | solution.py:246
  68.0 0.0 copy-start.5
  68.0 0.0 copy-done.3
  68.0 10.7 %collective-permute-start = (bf16[64,512]{1,0:T(8,128)(2,1)S(1)}, bf16[64,512]{1,0:T(8,128)(2,1)S(1)}, u32[]{:S(2)}, u32[]{:S(2)}) collective-permute-start(bf16[64,512]{1,0:T(8,128)(2,1)S(1)} %bitcast.19), channel_id=1, source_target_pairs={{0,4},{4,0},{1,5},{5,1},{2,6},{6,2},{3,7},{7,3},{8,12},{12,8},{9,1... | collective-permute-start | bytes 196616 | tf_op jit(solution)/shard_map/ppermute | solution.py:240
  78.7 0.9 collective-permute-done.partner_slab
  79.6 0.0 all-to-all-done.1.parts
  79.6 0.0 copy-done.4
  79.6 1.1 shard_map.65
  80.7 7.0 %all_to_all.26.parts = f32[4,24,128]{2,1,0:T(8,128)S(1)} all-to-all(f32[4,24,128]{2,1,0:T(8,128)S(1)} %shard_map.65), channel_id=1, replica_groups=mesh['y'=4,'z'=16,'c'=2,'x'=4] {'y'}, dimensions={0} | all-to-all | bytes 98304 | tf_op jit(solution)/shard_map/all_to_all | solution.py:256
  87.7 0.6 shard_map.66
  88.4 18.8 %all_to_all.27.parts = f32[16,24,128]{2,1,0:T(8,128)S(1)} all-to-all(f32[16,24,128]{2,1,0:T(8,128)S(1)} %broadcast_in_dim.10), channel_id=1, replica_groups=mesh['y'=4,'z'=16,'c'=2,'x'=4] {'z'}, dimensions={0} | all-to-all | bytes 393216 | tf_op jit(solution)/shard_map/all_to_all | solution.py:227
  107.2 0.7 shard_map.67
  108.0 22.9 %all_to_all.28 = f32[32,16,128]{2,1,0:T(8,128)S(1)} all-to-all(f32[32,16,128]{2,1,0:T(8,128)S(1)} %broadcast_in_dim.22), channel_id=1, replica_groups=mesh['y'=4,'z'=16,'c'=2,'x'=4] {'y','c','x'}, dimensions={0} | all-to-all | bytes 524288 | tf_op jit(solution)/shard_map/all_to_all | solution.py:227
  130.8 0.0 copy-done.5
  130.8 1.7 %shard_map.68 = f32[8,4096]{1,0:T(8,128)} custom-call(s32[4,128]{1,0:T(4,128)S(1)} %bitcast.22, f32[512,128]{1,0:T(8,128)S(1)} %bitcast.16), custom_call_target="tpu_custom_call" | custom-call | tf_op jit(solution)/shard_map/pallas_call | solution.py:195
  (2 shorter events, 0.0 us)
Async XLA Ops:
  0.0 58.7 %collective-permute-start.1 = (bf16[4096,512]{1,0:T(8,128)(2,1)}, bf16[4096,512]{1,0:T(8,128)(2,1)}, u32[]{:S(2)}, u32[]{:S(2)}) collective-permute-start(bf16[4096,512]{1,0:T(8,128)(2,1)} %own.1), channel_id=1, source_target_pairs={{0,4},{4,0},{1,5},{5,1},{2,6},{6,2},{3,7},{7,3},{8,12},{12,8},{9,1... | collective-permute-start | bytes 12582920 | tf_op jit(solution)/shard_map/ppermute | solution.py:239
  35.2 23.5 %copy-start.1 = (bf16[4096,64]{0,1:T(8,128)(2,1)S(1)}, bf16[4096,64]{0,1:T(8,128)(2,1)}, u32[]{:S(2)}) copy-start(bf16[4096,64]{0,1:T(8,128)(2,1)} %param.11) | copy-start | bytes 1572868
  35.2 23.5 %copy-start.2 = (bf16[4,4096]{1,0:T(4,128)(2,1)S(1)}, bf16[4,4096]{1,0:T(4,128)(2,1)}, u32[]{:S(2)}) copy-start(bf16[4,4096]{1,0:T(4,128)(2,1)} %hidden) | copy-start | bytes 98308
  35.5 23.2 %copy-start = (bf16[4096,512]{1,0:T(8,128)(2,1)S(1)}, bf16[4096,512]{1,0:T(8,128)(2,1)}, u32[]{:S(2)}) copy-start(bf16[4096,512]{1,0:T(8,128)(2,1)} %own.1) | copy-start | bytes 12582916
  63.9 4.2 %copy-start.3 = (bf16[512,64]{0,1:T(8,128)(2,1)S(1)}, bf16[512,64]{0,1:T(8,128)(2,1)}, u32[]{:S(2)}) copy-start(bf16[512,64]{0,1:T(8,128)(2,1)} %param.10) | copy-start | bytes 196612
  63.9 15.7 %copy-start.4 = (s32[512]{0:T(512)S(1)}, s32[512]{0:T(512)}, u32[]{:S(2)}) copy-start(s32[512]{0:T(512)} %param.8) | copy-start | bytes 6148
  63.9 15.7 %all-to-all-start.1 = ((f32[4,72,1024]{2,1,0:T(8,128)}), f32[4,72,1024]{2,1,0:T(8,128)S(1)}, u32[]{:S(2)}, u32[]{:S(2)}) async-start(f32[4,72,1024]{2,1,0:T(8,128)} %shard_map.64), calls=%async_computation.1 | async-start | bytes 2359296 | tf_op jit(solution)/shard_map/all_to_all | solution.py:246
  68.0 62.8 %copy-start.5 = (s32[512]{0:T(512)S(1)}, s32[512]{0:T(512)}, u32[]{:S(2)}) copy-start(s32[512]{0:T(512)} %param.9) | copy-start | bytes 6148
  68.0 11.5 %collective-permute-start = (bf16[64,512]{1,0:T(8,128)(2,1)S(1)}, bf16[64,512]{1,0:T(8,128)(2,1)S(1)}, u32[]{:S(2)}, u32[]{:S(2)}) collective-permute-start(bf16[64,512]{1,0:T(8,128)(2,1)S(1)} %bitcast.19), channel_id=1, source_target_pairs={{0,4},{4,0},{1,5},{5,1},{2,6},{6,2},{3,7},{7,3},{8,12},{12,8},{9,1... | collective-permute-start | bytes 196616 | tf_op jit(solution)/shard_map/ppermute | solution.py:240

commit v4 on v3

v4 whole, which is shorter than its diff:
```python
import functools

import jax
import jax.numpy as jnp
from jax import lax
from jax.experimental import pallas as pl
from jax.experimental.pallas import tpu as pltpu
from jax.sharding import Mesh
from jax.sharding import PartitionSpec as P

NY, NZ, NC, NX = 4, 16, 2, 4
SKETCH = 64
DOCS = 8
LANES = 128
F32 = jnp.float32
HIGHEST = lax.Precision.HIGHEST


def iota(shape, dim):
    return lax.broadcasted_iota(jnp.int32, shape, dim)


def softmax_kernel(place, targets, slabs, partner_slabs, parts, out):
    core, x, y, z = place[0], place[1], place[2], place[3]
    cols = slabs.shape[2]
    tiles = cols // LANES
    lane, row = iota((NZ, LANES), 1), iota((NZ, LANES), 0)
    hit = lane == row * (NC * NX) + (core * NX + x)
    target = jnp.sum(jnp.where(hit, targets[pl.ds(y, 1), :], 0), axis=1, keepdims=True)
    blocks = []
    for source in range(NY):
        every = functools.reduce(jnp.add, [parts[source * NX + i, : 2 * tiles * NZ] for i in range(NX)])
        for side in range(NC):
            owner = core if side == 0 else 1 - core
            pieces = [every[(side * tiles + t) * NZ :][:NZ] for t in range(tiles)]
            first = ((source * NZ + z) * NC + owner) * cols
            slab = (partner_slabs if side else slabs)[source]
            blocks.append((jnp.concatenate(pieces, axis=1), slab, first))
    tops = [jnp.max(logits, axis=1, keepdims=True) for logits, _, _ in blocks]
    top = functools.reduce(jnp.maximum, tops)
    total = target_logit = sketches = 0.0
    for logits, slab, first in blocks:
        is_target = iota(logits.shape, 1) + first == target
        exponent = jnp.exp(logits - top)
        total += jnp.sum(exponent, axis=1, keepdims=True)
        target_logit += jnp.sum(jnp.where(is_target, logits, 0.0), axis=1, keepdims=True)
        high, low = halves(jnp.where(is_target, 0.0, exponent))
        stacked = jnp.concatenate([high, low, is_target.astype(F32).astype(jnp.bfloat16)], axis=0)
        sketches += lax.dot_general(
            stacked, slab, (((1,), (1,)), ((), ())), preferred_element_type=F32
        )
    both = jnp.concatenate([sketches[:NZ] + sketches[NZ : 2 * NZ], sketches[2 * NZ :]], axis=1)
    feat = jnp.zeros((8, LANES), F32)
    for i in range(NX):
        feat = feat + parts[y * NX + i, 2 * tiles * NZ :]
    pack(both, (top, total, target_logit), feat, out)


def pack(both, columns, feat, out):
    left = iota((NZ, LANES), 1) < SKETCH
    spot = iota((NZ, LANES), 1) == iota((NZ, LANES), 0) + SKETCH
    lines = []
    for column in columns:
        lines += thirds(jnp.sum(jnp.where(spot, column, 0.0), axis=0, keepdims=True))
    lines += thirds(pltpu.roll(feat, SKETCH, 1)[:1])[:2]
    index = iota((NZ, LANES), 0)
    second = both - both.astype(jnp.bfloat16).astype(F32)
    other = jnp.zeros((NZ, LANES), F32)
    for i, line in enumerate(lines):
        other = jnp.where(index == i, line, other)
    out[:, :LANES] = both.astype(jnp.bfloat16)
    out[:, LANES:] = jnp.where(left, second, other).astype(jnp.bfloat16)


def thirds(a):
    high = a.astype(jnp.bfloat16).astype(F32)
    mid = (a - high).astype(jnp.bfloat16).astype(F32)
    return [high, mid, a - high - mid]


def finish_kernel(parts, out):
    boths = [(parts[z, :, :LANES].astype(F32), parts[z, :, LANES:].astype(F32)) for z in range(NZ)]
    stats = [
        [low[k : k + 1] + low[k + 1 : k + 2] + low[k + 2 : k + 3] for k in (0, 3, 6)] for _, low in boths
    ]
    top = functools.reduce(jnp.maximum, [s[0] for s in stats])
    scales = [jnp.exp(s[0] - top) for s in stats]
    lane, row = iota((NZ, LANES), 1), iota((NZ, LANES), 0)
    left, mine = lane < SKETCH, lane == row + SKETCH

    def as_column(line):
        return jnp.sum(jnp.where(mine, line, 0.0), axis=1, keepdims=True)

    total = as_column(sum(scale * s[1] for scale, s in zip(scales, stats)))
    target_logit = as_column(sum(s[2] for s in stats))
    both = jnp.zeros((NZ, LANES), F32)
    for (high, low), scale in zip(boths, scales):
        both = both + jnp.where(left, (high + low) * as_column(scale), high)
    chance = jnp.exp(target_logit - as_column(top)) / total
    weight = (chance - 1.0).astype(jnp.bfloat16).astype(F32)
    grad = both / total + weight * pltpu.roll(both, SKETCH, 1)
    feat = sum(jnp.where(row == z, low[9:10] + low[10:11], 0.0) for z, (_, low) in enumerate(boths))
    out[...] = jnp.where(left, grad, feat)


def halves(a):
    high = a.astype(jnp.bfloat16)
    return high, (a - high.astype(F32)).astype(jnp.bfloat16)


def document_kernel(segments, rows, out):
    tokens, half = rows.shape[0], SKETCH * DOCS // 2
    values = rows[...]
    index = iota((1, tokens), 1)
    y, c, x, z = index // 128, (index // 64) % 2, (index // 16) % 4, index % 16
    token = y * 128 + z * 8 + c * 4 + x
    segment = segments[...]
    doc = iota((half, 1), 0) % DOCS
    start = jnp.zeros((half, 1), jnp.int32)
    stop = jnp.zeros((half, 1), jnp.int32)
    inverse = jnp.zeros((DOCS, LANES), F32)
    below = jnp.zeros((1, 1), jnp.int32)
    for s in range(DOCS):
        here = jnp.sum(
            jnp.sum((segment == s).astype(jnp.int32), axis=1, keepdims=True), axis=0, keepdims=True
        )
        start = jnp.where(doc == s, below, start)
        below = below + here
        stop = jnp.where(doc == s, below, stop)
        inverse = jnp.where(iota((DOCS, LANES), 0) == s, 1.0 / jnp.sqrt(here.astype(F32)), inverse)
    member = (token >= start) & (token < stop)
    left = iota((tokens, LANES), 1) < SKETCH
    swapped = pltpu.roll(values, SKETCH, 1)
    grad = halves(values)
    total = jnp.zeros((half, LANES), F32)
    for odd in range(2):
        pick = iota((half, LANES), 1) == 2 * (iota((half, LANES), 0) // DOCS) + odd
        pick = pick.astype(F32).astype(jnp.bfloat16)
        spread = [
            lax.dot_general(pick, g, (((1,), (1,)), ((), ())), preferred_element_type=F32)
            for g in grad
        ]
        high, low = [jnp.where(member, a, 0.0).astype(jnp.bfloat16) for a in spread]
        feat_high, feat_low = halves(jnp.where(left, 0.0, values) if odd else jnp.where(left, swapped, 0.0))
        for a, b in ((high, feat_high), (high, feat_low), (low, feat_high)):
            total = total + jnp.dot(a, b, preferred_element_type=F32)
    for pair in range(SKETCH // 2):
        out[:, pair * LANES : (pair + 1) * LANES] = total[pair * DOCS : (pair + 1) * DOCS] * inverse


def logits_kernel(rows, own, partner, hidden, feature_slab, out, weights, total, staged, sems, out_sems):
    steps = sems.shape[0]
    depth, cols = own.shape[0] // steps, own.shape[1]
    copies = []
    for k in range(steps):
        part = pl.ds(k * depth, depth)
        copies.append(pltpu.make_async_copy(partner.at[part], weights.at[part], sems.at[k]))
    for copy in copies:
        copy.start()
    tiles = 2 * cols // LANES
    quarter = lax.dot_general(
        hidden[...], feature_slab[...], (((1,), (1,)), ((), ())), preferred_element_type=F32
    )
    feat = jnp.concatenate([quarter, jnp.zeros((NX, LANES - SKETCH), F32)], axis=1)
    for y in range(NY):
        for j in range(NX):
            staged[y * NX + j, tiles * NZ :, :] = jnp.broadcast_to(feat[j : j + 1], (8, LANES))
    for k in range(steps):
        part = pl.ds(k * depth, depth)
        left = jnp.dot(rows[:, part], own[part, :], preferred_element_type=F32)
        copies[k].wait()
        right = jnp.dot(rows[:, part], weights[part, :], preferred_element_type=F32)
        term = jnp.concatenate([left, right], axis=1)
        if k == 0:
            total[...] = term
        elif k < steps - 1:
            total[...] += term
    sends = []
    for y in range(NY):
        for j in range(NX):
            block = y * NX + j
            piece = total[block * NZ : (block + 1) * NZ, :] + term[block * NZ : (block + 1) * NZ]
            for t in range(tiles):
                staged[block, t * NZ : (t + 1) * NZ, :] = piece[:, t * LANES : (t + 1) * LANES]
        part = pl.ds(y * NX, NX)
        sends.append(pltpu.make_async_copy(staged.at[part], out.at[part], out_sems.at[y]))
        sends[y].start()
    for send in sends:
        send.wait()


def call(kernel, shape, *args, dtype=F32):
    vmem = pl.BlockSpec(memory_space=pltpu.VMEM)
    smem = pl.BlockSpec(memory_space=pltpu.SMEM)
    return pl.pallas_call(
        kernel,
        out_shape=jax.ShapeDtypeStruct(shape, dtype),
        in_specs=[smem if a.ndim == 1 else vmem for a in args],
        out_specs=vmem,
        compiler_params=pltpu.CompilerParams(vmem_limit_bytes=16 * 1024 * 1024),
    )(*args)


def all_logits(rows, own, partner, hidden, feature_slab):
    vmem = pl.BlockSpec(memory_space=pltpu.VMEM)
    far = pl.BlockSpec(memory_space=pltpu.HBM)
    width, cols = own.shape
    shape = (NY * NX, NZ * 2 * cols // LANES + 8, LANES)
    return pl.pallas_call(
        logits_kernel,
        out_shape=jax.ShapeDtypeStruct(shape, F32),
        in_specs=[vmem, vmem, far, vmem, vmem],
        out_specs=far,
        scratch_shapes=[
            pltpu.VMEM((width, cols), own.dtype),
            pltpu.VMEM((rows.shape[0], 2 * cols), F32),
            pltpu.VMEM(shape, F32),
            pltpu.SemaphoreType.DMA((4,)),
            pltpu.SemaphoreType.DMA((NY,)),
        ],
        compiler_params=pltpu.CompilerParams(vmem_limit_bytes=32 * 1024 * 1024),
    )(rows, own, partner, hidden, feature_slab)


def to_all(block, axes, count):
    copies = jnp.broadcast_to(block[None], (count,) + block.shape)
    return lax.all_to_all(copies, axes, 0, 0, tiled=True)


def on_device(hidden, head, targets, segment_ids, grad_slab, feature_slab):
    y, c, x = lax.axis_index("y"), lax.axis_index("c"), lax.axis_index("x")
    z = lax.axis_index("z")
    width = hidden.shape[1]
    place = jnp.stack([c, x, y, z]).astype(jnp.int32)
    hidden, place = lax.optimization_barrier((hidden, place))
    partner_head = lax.ppermute(head, "c", [(0, 1), (1, 0)])
    column = lax.all_gather(hidden, "z")
    column = column.transpose(1, 0, 2).reshape(NX * NZ, width)
    beside = jnp.concatenate([column, grad_slab.T], axis=1)
    rows = to_all(beside, "y", NY)
    slabs = rows[:, :, width:]
    rows = rows.reshape(NY * NX * NZ, -1)
    outgoing = all_logits(rows, head, partner_head, hidden, feature_slab.T)
    slabs, outgoing = lax.optimization_barrier((slabs, outgoing))
    partner_slabs = lax.ppermute(slabs, "c", [(0, 1), (1, 0)])
    parts = lax.all_to_all(outgoing, ("y", "x"), 0, 0, tiled=True)
    chunk = call(
        softmax_kernel,
        (NZ, 2 * LANES),
        place,
        targets.reshape(NY, LANES),
        slabs,
        partner_slabs,
        parts,
        dtype=jnp.bfloat16,
    )
    rows = call(finish_kernel, (NZ, LANES), to_all(chunk, "z", NZ))
    everyone = to_all(rows, ("y", "c", "x"), NY * NC * NX).reshape(-1, LANES)
    return call(
        document_kernel,
        (DOCS, SKETCH * SKETCH),
        segment_ids.reshape(NY, LANES),
        everyone,
    )


def solution(mesh):
    fine = Mesh(mesh.devices.reshape(NY, NZ, NC, NX), ("y", "z", "c", "x"))
    vocab = ("y", "z", "c")
    return jax.shard_map(
        on_device,
        mesh=fine,
        in_specs=(P(vocab, "x"), P("x", vocab), P(), P(), P(vocab, None), P("x", None)),
        out_specs=P(),
        check_vma=False,
    )
```

time: 133 us -> 129 us (0.970)
  blocking collectives: 98 us -> 93.6 us
  Pallas kernels: 9.24 us -> 7.5 us
    all_to_all x1 -> x0, blocking collectives: 7.04 us -> none  [on_device(): chunks = lax.all_to_all(chunks, 'y', 0, 0, tiled=True)]
    all_to_all x3, blocking collectives: 64.9 us -> 67.5 us  [to_all(): return lax.all_to_all(copies, axes, 0, 0, tiled=True)]
    pallas_call x4 -> x3, Pallas kernels: 4.12 us -> 2.93 us  [call(): pl.pallas_call(kernel, out_shape=jax.ShapeDtypeStruct(shape, dtype), in_s...]
  transfers between devices with their start and end apart: 3 -> 3, of which waited for: 1 -> 2; matrix products, arithmetic and copies ran while one was open for 0% -> 0% of each run, Pallas kernels for 0% -> 0%
where the time goes in v4:
time: 129 us; the launch traced here: 128 us
  blocking collectives  93.6 us (73%)
  starting transfers between devices  24.2 us (19%)
  Pallas kernels  7.5 us (6%)
  waiting for transfers between devices  2.1 us (2%)
    all_to_all x3, blocking collectives, to_all(): return lax.all_to_all(copies, axes, 0, 0, tiled=True)  67.5 us
    all_gather x1, blocking collectives, on_device(): column = lax.all_gather(hidden, 'z')  26.1 us
    ppermute x1, starting transfers between devices, on_device(): partner_slabs = lax.ppermute(slabs, 'c', [(0, 1), (1, 0)])  10.5 us
    ppermute x1, starting transfers between devices, on_device(): partner_head = lax.ppermute(head, 'c', [(0, 1), (1, 0)])  8.91 us
    all_to_all x1, starting transfers between devices, on_device(): parts = lax.all_to_all(outgoing, ('y', 'x'), 0, 0, tiled=True)  4.74 us
    pallas_call x1, Pallas kernels, all_logits(): pl.pallas_call(logits_kernel, out_shape=jax.ShapeDtypeStruct(shape, F32),...  4.57 us
    pallas_call x3, Pallas kernels, call(): pl.pallas_call(kernel, out_shape=jax.ShapeDtypeStruct(shape, dtype), in_s...  2.93 us
  transfers between devices with their start and end apart: 3, of which 2 were waited for; matrix products, arithmetic and copies ran while one was open for 0% of the time, Pallas kernels for 0%

profile of v4, /device:TPU:1, one launch (start us, length us, event | category | flops | bytes accessed | tf_op | source)
XLA Modules:
  0.0 128.2 jit_solution(5694930908553998164)
XLA Ops:
  0.0 0.0 copy-start.5
  0.0 8.9 %collective-permute-start = (bf16[4096,512]{1,0:T(8,128)(2,1)}, bf16[4096,512]{1,0:T(8,128)(2,1)}, u32[]{:S(2)}, u32[]{:S(2)}) collective-permute-start(bf16[4096,512]{1,0:T(8,128)(2,1)} %own.1), channel_id=1, source_target_pairs={{0,4},{4,0},{1,5},{5,1},{2,6},{6,2},{3,7},{7,3},{8,12},{12,8},{9,1... | collective-permute-start | bytes 12582920 | tf_op jit(solution)/shard_map/ppermute | solution.py:236
  8.9 0.1 pad_add_fusion.place
  9.0 26.1 %all-gather.1 = bf16[16,4,4096]{2,1,0:T(4,128)(2,1)S(1)} all-gather(bf16[1,4,4096]{2,1,0:T(4,128)(2,1)} %bitcast.17), channel_id=2, replica_groups=mesh['y'=4,'z'=16,'c'=2,'x'=4] {'z'}, dimensions={0}, use_global_device_ids=true | all-gather | bytes 557056 | tf_op jit(solution)/shard_map/all_gather | solution.py:237
  35.1 0.3 copy.8
  35.4 0.0 copy-done.5
  35.4 0.2 broadcast_in_dim.6
  35.6 0.0 copy-start
  35.6 0.0 copy-start.1
  35.6 0.0 copy-start.2
  35.6 26.0 %all_to_all.20 = bf16[4,64,4608]{2,1,0:T(8,128)(2,1)S(1)} all-to-all(bf16[4,64,4608]{2,1,0:T(8,128)(2,1)S(1)} %broadcast_in_dim.6), channel_id=1, replica_groups=mesh['y'=4,'z'=16,'c'=2,'x'=4] {'y'}, dimensions={0} | all-to-all | bytes 4718592 | tf_op jit(solution)/shard_map/all_to_all | solution.py:227
  61.7 0.0 collective-permute-done.partner
  61.7 0.0 copy-done
  61.7 0.0 copy-done.1
  61.7 0.0 copy-done.2
  61.7 4.6 %shard_map.64 = f32[16,136,128]{2,1,0:T(8,128)} custom-call(bf16[256,4608]{1,0:T(8,128)(2,1)S(1)} %bitcast.14, bf16[4096,512]{1,0:T(8,128)(2,1)S(1)} %copy-done, bf16[4096,512]{1,0:T(8,128)(2,1)} %collective-permute-done.partner, bf16[4,4096]{1,0:T(4,128)(2,1)S(1)} %copy-done.2, bf16[64,4096]{1,0:T(8,128)(2,1)S(1)} %bitcast.16), custom_call_target="tpu_custom_call" | custom-call | tf_op jit(solution)/shard_map/pallas_call | solution.py:209
  66.3 0.0 copy-start.3
  66.3 4.7 %all-to-all-start.1 = ((f32[16,136,128]{2,1,0:T(8,128)}), f32[16,136,128]{2,1,0:T(8,128)S(1)}, u32[]{:S(2)}, u32[]{:S(2)}) async-start(f32[16,136,128]{2,1,0:T(8,128)} %shard_map.64), calls=%async_computation.1 | async-start | bytes 2228224 | tf_op jit(solution)/shard_map/all_to_all | solution.py:246
  71.0 10.5 %collective-permute-start.1 = (bf16[4,64,512]{2,1,0:T(8,128)(2,1)S(1)}, bf16[4,64,512]{2,1,0:T(8,128)(2,1)S(1)}, u32[]{:S(2)}, u32[]{:S(2)}) collective-permute-start(bf16[4,64,512]{2,1,0:T(8,128)(2,1)S(1)} %slice.4.slabs), channel_id=1, source_target_pairs={{0,4},{4,0},{1,5},{5,1},{2,6},{6,2},{3,7},{7,3},{8,12},{12,8},{9,1... | collective-permute-start | bytes 786440 | tf_op jit(solution)/shard_map/ppermute | solution.py:245
  81.6 1.1 collective-permute-done.1.partner_slabs
  82.7 1.0 all-to-all-done.1.parts
  83.7 0.0 copy-done.3
  83.7 0.0 copy-start.4
  83.7 1.0 shard_map.65
  84.7 18.7 %all_to_all.21.parts = bf16[16,16,256]{2,1,0:T(8,128)(2,1)S(1)} all-to-all(bf16[16,16,256]{2,1,0:T(8,128)(2,1)S(1)} %broadcast_in_dim.7), channel_id=1, replica_groups=mesh['y'=4,'z'=16,'c'=2,'x'=4] {'z'}, dimensions={0} | all-to-all | bytes 262144 | tf_op jit(solution)/shard_map/all_to_all | solution.py:227
  103.4 0.2 shard_map.66
  103.6 22.9 %all_to_all.22 = f32[32,16,128]{2,1,0:T(8,128)S(1)} all-to-all(f32[32,16,128]{2,1,0:T(8,128)S(1)} %broadcast_in_dim.8), channel_id=1, replica_groups=mesh['y'=4,'z'=16,'c'=2,'x'=4] {'y','c','x'}, dimensions={0} | all-to-all | bytes 524288 | tf_op jit(solution)/shard_map/all_to_all | solution.py:227
  126.5 0.0 copy-done.4
  126.5 1.7 %shard_map.67 = f32[8,4096]{1,0:T(8,128)} custom-call(s32[4,128]{1,0:T(4,128)S(1)} %bitcast.19, f32[512,128]{1,0:T(8,128)S(1)} %bitcast.15), custom_call_target="tpu_custom_call" | custom-call | tf_op jit(solution)/shard_map/pallas_call | solution.py:195
  (4 shorter events, 0.1 us)
Async XLA Ops:
  0.0 35.4 %copy-start.5 = (bf16[512,64]{0,1:T(8,128)(2,1)S(1)}, bf16[512,64]{0,1:T(8,128)(2,1)}, u32[]{:S(2)}) copy-start(bf16[512,64]{0,1:T(8,128)(2,1)} %param.10) | copy-start | bytes 196612
  0.0 61.7 %collective-permute-start = (bf16[4096,512]{1,0:T(8,128)(2,1)}, bf16[4096,512]{1,0:T(8,128)(2,1)}, u32[]{:S(2)}, u32[]{:S(2)}) collective-permute-start(bf16[4096,512]{1,0:T(8,128)(2,1)} %own.1), channel_id=1, source_target_pairs={{0,4},{4,0},{1,5},{5,1},{2,6},{6,2},{3,7},{7,3},{8,12},{12,8},{9,1... | collective-permute-start | bytes 12582920 | tf_op jit(solution)/shard_map/ppermute | solution.py:236
  35.6 26.1 %copy-start = (bf16[4096,512]{1,0:T(8,128)(2,1)S(1)}, bf16[4096,512]{1,0:T(8,128)(2,1)}, u32[]{:S(2)}) copy-start(bf16[4096,512]{1,0:T(8,128)(2,1)} %own.1) | copy-start | bytes 12582916
  35.6 26.1 %copy-start.1 = (bf16[4096,64]{0,1:T(8,128)(2,1)S(1)}, bf16[4096,64]{0,1:T(8,128)(2,1)}, u32[]{:S(2)}) copy-start(bf16[4096,64]{0,1:T(8,128)(2,1)} %param.11) | copy-start | bytes 1572868
  35.6 26.1 %copy-start.2 = (bf16[4,4096]{1,0:T(4,128)(2,1)S(1)}, bf16[4,4096]{1,0:T(4,128)(2,1)}, u32[]{:S(2)}) copy-start(bf16[4,4096]{1,0:T(4,128)(2,1)} %hidden) | copy-start | bytes 98308
  66.3 17.4 %copy-start.3 = (s32[512]{0:T(512)S(1)}, s32[512]{0:T(512)}, u32[]{:S(2)}) copy-start(s32[512]{0:T(512)} %param.8) | copy-start | bytes 6148
  66.3 17.4 %all-to-all-start.1 = ((f32[16,136,128]{2,1,0:T(8,128)}), f32[16,136,128]{2,1,0:T(8,128)S(1)}, u32[]{:S(2)}, u32[]{:S(2)}) async-start(f32[16,136,128]{2,1,0:T(8,128)} %shard_map.64), calls=%async_computation.1 | async-start | bytes 2228224 | tf_op jit(solution)/shard_map/all_to_all | solution.py:246
  71.0 11.7 %collective-permute-start.1 = (bf16[4,64,512]{2,1,0:T(8,128)(2,1)S(1)}, bf16[4,64,512]{2,1,0:T(8,128)(2,1)S(1)}, u32[]{:S(2)}, u32[]{:S(2)}) collective-permute-start(bf16[4,64,512]{2,1,0:T(8,128)(2,1)S(1)} %slice.4.slabs), channel_id=1, source_target_pairs={{0,4},{4,0},{1,5},{5,1},{2,6},{6,2},{3,7},{7,3},{8,12},{12,8},{9,1... | collective-permute-start | bytes 786440 | tf_op jit(solution)/shard_map/ppermute | solution.py:245
  83.7 42.8 %copy-start.4 = (s32[512]{0:T(512)S(1)}, s32[512]{0:T(512)}, u32[]{:S(2)}) copy-start(s32[512]{0:T(512)} %param.9) | copy-start | bytes 6148

commit v5 on v4

--- a/solution.py
+++ b/solution.py
@@ -165,26 +165,28 @@
     for y in range(NY):
         for j in range(NX):
             staged[y * NX + j, tiles * NZ :, :] = jnp.broadcast_to(feat[j : j + 1], (8, LANES))
-    for k in range(steps):
-        part = pl.ds(k * depth, depth)
-        left = jnp.dot(rows[:, part], own[part, :], preferred_element_type=F32)
-        copies[k].wait()
-        right = jnp.dot(rows[:, part], weights[part, :], preferred_element_type=F32)
-        term = jnp.concatenate([left, right], axis=1)
-        if k == 0:
-            total[...] = term
-        elif k < steps - 1:
-            total[...] += term
     sends = []
-    for y in range(NY):
-        for j in range(NX):
-            block = y * NX + j
-            piece = total[block * NZ : (block + 1) * NZ, :] + term[block * NZ : (block + 1) * NZ]
-            for t in range(tiles):
-                staged[block, t * NZ : (t + 1) * NZ, :] = piece[:, t * LANES : (t + 1) * LANES]
-        part = pl.ds(y * NX, NX)
-        sends.append(pltpu.make_async_copy(staged.at[part], out.at[part], out_sems.at[y]))
-        sends[y].start()
+    side_rows = tiles * NZ // 2
+    for side, head in enumerate((own, weights)):
+        for k in range(steps):
+            if side:
+                copies[k].wait()
+            part = pl.ds(k * depth, depth)
+            term = jnp.dot(rows[:, part], head[part, :], preferred_element_type=F32)
+            total[...] = total[...] + term if k else term
+        for y in range(NY):
+            for j in range(NX):
+                block = y * NX + j
+                piece = total[block * NZ : (block + 1) * NZ, :]
+                for t in range(tiles // 2):
+                    first = side * side_rows + t * NZ
+                    staged[block, first : first + NZ, :] = piece[:, t * LANES : (t + 1) * LANES]
+            blocks = pl.ds(y * NX, NX)
+            span = pl.ds(side * side_rows, side_rows + 8 * side)
+            sends.append(
+                pltpu.make_async_copy(staged.at[blocks, span], out.at[blocks, span], out_sems.at[side, y])
+            )
+            sends[-1].start()
     for send in sends:
         send.wait()
 
@@ -213,10 +215,10 @@
         out_specs=far,
         scratch_shapes=[
             pltpu.VMEM((width, cols), own.dtype),
-            pltpu.VMEM((rows.shape[0], 2 * cols), F32),
+            pltpu.VMEM((rows.shape[0], cols), F32),
             pltpu.VMEM(shape, F32),
             pltpu.SemaphoreType.DMA((4,)),
-            pltpu.SemaphoreType.DMA((NY,)),
+            pltpu.SemaphoreType.DMA((2, NY)),
         ],
         compiler_params=pltpu.CompilerParams(vmem_limit_bytes=32 * 1024 * 1024),
     )(rows, own, partner, hidden, feature_slab)

time: 129 us -> 128 us (level)
  no operation moved by 1% of the time
where the time goes in v5:
time: 128 us; the launch traced here: 127 us
  blocking collectives  93.6 us (73%)
  starting transfers between devices  24.2 us (19%)
  Pallas kernels  6.59 us (5%)
  waiting for transfers between devices  2.09 us (2%)
    all_to_all x3, blocking collectives, to_all(): return lax.all_to_all(copies, axes, 0, 0, tiled=True)  67.5 us
    all_gather x1, blocking collectives, on_device(): column = lax.all_gather(hidden, 'z')  26.1 us
    ppermute x1, starting transfers between devices, on_device(): partner_slabs = lax.ppermute(slabs, 'c', [(0, 1), (1, 0)])  10.5 us
    ppermute x1, starting transfers between devices, on_device(): partner_head = lax.ppermute(head, 'c', [(0, 1), (1, 0)])  8.91 us
    all_to_all x1, starting transfers between devices, on_device(): parts = lax.all_to_all(outgoing, ('y', 'x'), 0, 0, tiled=True)  4.74 us
    pallas_call x1, Pallas kernels, all_logits(): pl.pallas_call(logits_kernel, out_shape=jax.ShapeDtypeStruct(shape, F32),...  3.66 us
    pallas_call x3, Pallas kernels, call(): pl.pallas_call(kernel, out_shape=jax.ShapeDtypeStruct(shape, dtype), in_s...  2.94 us
  transfers between devices with their start and end apart: 3, of which 2 were waited for; matrix products, arithmetic and copies ran while one was open for 0% of the time, Pallas kernels for 0%

profile of v5, /device:TPU:1, one launch (start us, length us, event | category | flops | bytes accessed | tf_op | source)
XLA Modules:
  0.0 127.3 jit_solution(12257382030920846851)
XLA Ops:
  0.0 0.0 copy-start.5
  0.0 8.9 %collective-permute-start = (bf16[4096,512]{1,0:T(8,128)(2,1)}, bf16[4096,512]{1,0:T(8,128)(2,1)}, u32[]{:S(2)}, u32[]{:S(2)}) collective-permute-start(bf16[4096,512]{1,0:T(8,128)(2,1)} %own.1), channel_id=1, source_target_pairs={{0,4},{4,0},{1,5},{5,1},{2,6},{6,2},{3,7},{7,3},{8,12},{12,8},{9,1... | collective-permute-start | bytes 12582920 | tf_op jit(solution)/shard_map/ppermute | solution.py:238
  8.9 0.1 pad_add_fusion.place
  9.0 26.1 %all-gather.1 = bf16[16,4,4096]{2,1,0:T(4,128)(2,1)S(1)} all-gather(bf16[1,4,4096]{2,1,0:T(4,128)(2,1)} %bitcast.17), channel_id=2, replica_groups=mesh['y'=4,'z'=16,'c'=2,'x'=4] {'z'}, dimensions={0}, use_global_device_ids=true | all-gather | bytes 557056 | tf_op jit(solution)/shard_map/all_gather | solution.py:239
  35.1 0.3 copy.8
  35.4 0.0 copy-done.5
  35.4 0.2 broadcast_in_dim.6
  35.6 0.0 copy-start
  35.6 0.0 copy-start.1
  35.6 0.0 copy-start.2
  35.6 26.0 %all_to_all.20 = bf16[4,64,4608]{2,1,0:T(8,128)(2,1)S(1)} all-to-all(bf16[4,64,4608]{2,1,0:T(8,128)(2,1)S(1)} %broadcast_in_dim.6), channel_id=1, replica_groups=mesh['y'=4,'z'=16,'c'=2,'x'=4] {'y'}, dimensions={0} | all-to-all | bytes 4718592 | tf_op jit(solution)/shard_map/all_to_all | solution.py:229
  61.7 0.0 collective-permute-done.partner
  61.7 0.0 copy-done
  61.7 0.0 copy-done.1
  61.7 0.0 copy-done.2
  61.7 3.7 %shard_map.64 = f32[16,136,128]{2,1,0:T(8,128)} custom-call(bf16[256,4608]{1,0:T(8,128)(2,1)S(1)} %bitcast.14, bf16[4096,512]{1,0:T(8,128)(2,1)S(1)} %copy-done, bf16[4096,512]{1,0:T(8,128)(2,1)} %collective-permute-done.partner, bf16[4,4096]{1,0:T(4,128)(2,1)S(1)} %copy-done.2, bf16[64,4096]{1,0:T(8,128)(2,1)S(1)} %bitcast.16), custom_call_target="tpu_custom_call" | custom-call | tf_op jit(solution)/shard_map/pallas_call | solution.py:211
  65.4 0.0 copy-start.3
  65.4 4.7 %all-to-all-start.1 = ((f32[16,136,128]{2,1,0:T(8,128)}), f32[16,136,128]{2,1,0:T(8,128)S(1)}, u32[]{:S(2)}, u32[]{:S(2)}) async-start(f32[16,136,128]{2,1,0:T(8,128)} %shard_map.64), calls=%async_computation.1 | async-start | bytes 2228224 | tf_op jit(solution)/shard_map/all_to_all | solution.py:248
  70.1 10.5 %collective-permute-start.1 = (bf16[4,64,512]{2,1,0:T(8,128)(2,1)S(1)}, bf16[4,64,512]{2,1,0:T(8,128)(2,1)S(1)}, u32[]{:S(2)}, u32[]{:S(2)}) collective-permute-start(bf16[4,64,512]{2,1,0:T(8,128)(2,1)S(1)} %slice.4.slabs), channel_id=1, source_target_pairs={{0,4},{4,0},{1,5},{5,1},{2,6},{6,2},{3,7},{7,3},{8,12},{12,8},{9,1... | collective-permute-start | bytes 786440 | tf_op jit(solution)/shard_map/ppermute | solution.py:247
  80.7 1.1 collective-permute-done.1.partner_slabs
  81.8 0.9 all-to-all-done.1.parts
  82.8 0.0 copy-done.3
  82.8 0.0 copy-start.4
  82.8 1.0 shard_map.65
  83.8 18.7 %all_to_all.21.parts = bf16[16,16,256]{2,1,0:T(8,128)(2,1)S(1)} all-to-all(bf16[16,16,256]{2,1,0:T(8,128)(2,1)S(1)} %broadcast_in_dim.7), channel_id=1, replica_groups=mesh['y'=4,'z'=16,'c'=2,'x'=4] {'z'}, dimensions={0} | all-to-all | bytes 262144 | tf_op jit(solution)/shard_map/all_to_all | solution.py:229
  102.5 0.2 shard_map.66
  102.7 22.9 %all_to_all.22 = f32[32,16,128]{2,1,0:T(8,128)S(1)} all-to-all(f32[32,16,128]{2,1,0:T(8,128)S(1)} %broadcast_in_dim.8), channel_id=1, replica_groups=mesh['y'=4,'z'=16,'c'=2,'x'=4] {'y','c','x'}, dimensions={0} | all-to-all | bytes 524288 | tf_op jit(solution)/shard_map/all_to_all | solution.py:229
  125.6 0.0 copy-done.4
  125.6 1.7 %shard_map.67 = f32[8,4096]{1,0:T(8,128)} custom-call(s32[4,128]{1,0:T(4,128)S(1)} %bitcast.19, f32[512,128]{1,0:T(8,128)S(1)} %bitcast.15), custom_call_target="tpu_custom_call" | custom-call | tf_op jit(solution)/shard_map/pallas_call | solution.py:197
  (4 shorter events, 0.1 us)
Async XLA Ops:
  0.0 35.4 %copy-start.5 = (bf16[512,64]{0,1:T(8,128)(2,1)S(1)}, bf16[512,64]{0,1:T(8,128)(2,1)}, u32[]{:S(2)}) copy-start(bf16[512,64]{0,1:T(8,128)(2,1)} %param.10) | copy-start | bytes 196612
  0.0 61.7 %collective-permute-start = (bf16[4096,512]{1,0:T(8,128)(2,1)}, bf16[4096,512]{1,0:T(8,128)(2,1)}, u32[]{:S(2)}, u32[]{:S(2)}) collective-permute-start(bf16[4096,512]{1,0:T(8,128)(2,1)} %own.1), channel_id=1, source_target_pairs={{0,4},{4,0},{1,5},{5,1},{2,6},{6,2},{3,7},{7,3},{8,12},{12,8},{9,1... | collective-permute-start | bytes 12582920 | tf_op jit(solution)/shard_map/ppermute | solution.py:238
  35.6 26.1 %copy-start = (bf16[4096,512]{1,0:T(8,128)(2,1)S(1)}, bf16[4096,512]{1,0:T(8,128)(2,1)}, u32[]{:S(2)}) copy-start(bf16[4096,512]{1,0:T(8,128)(2,1)} %own.1) | copy-start | bytes 12582916
  35.6 26.1 %copy-start.1 = (bf16[4096,64]{0,1:T(8,128)(2,1)S(1)}, bf16[4096,64]{0,1:T(8,128)(2,1)}, u32[]{:S(2)}) copy-start(bf16[4096,64]{0,1:T(8,128)(2,1)} %param.11) | copy-start | bytes 1572868
  35.6 26.1 %copy-start.2 = (bf16[4,4096]{1,0:T(4,128)(2,1)S(1)}, bf16[4,4096]{1,0:T(4,128)(2,1)}, u32[]{:S(2)}) copy-start(bf16[4,4096]{1,0:T(4,128)(2,1)} %hidden) | copy-start | bytes 98308
  65.4 17.4 %copy-start.3 = (s32[512]{0:T(512)S(1)}, s32[512]{0:T(512)}, u32[]{:S(2)}) copy-start(s32[512]{0:T(512)} %param.8) | copy-start | bytes 6148
  65.4 17.4 %all-to-all-start.1 = ((f32[16,136,128]{2,1,0:T(8,128)}), f32[16,136,128]{2,1,0:T(8,128)S(1)}, u32[]{:S(2)}, u32[]{:S(2)}) async-start(f32[16,136,128]{2,1,0:T(8,128)} %shard_map.64), calls=%async_computation.1 | async-start | bytes 2228224 | tf_op jit(solution)/shard_map/all_to_all | solution.py:248
  70.1 11.7 %collective-permute-start.1 = (bf16[4,64,512]{2,1,0:T(8,128)(2,1)S(1)}, bf16[4,64,512]{2,1,0:T(8,128)(2,1)S(1)}, u32[]{:S(2)}, u32[]{:S(2)}) collective-permute-start(bf16[4,64,512]{2,1,0:T(8,128)(2,1)S(1)} %slice.4.slabs), channel_id=1, source_target_pairs={{0,4},{4,0},{1,5},{5,1},{2,6},{6,2},{3,7},{7,3},{8,12},{12,8},{9,1... | collective-permute-start | bytes 786440 | tf_op jit(solution)/shard_map/ppermute | solution.py:247
  82.8 42.8 %copy-start.4 = (s32[512]{0:T(512)S(1)}, s32[512]{0:T(512)}, u32[]{:S(2)}) copy-start(s32[512]{0:T(512)} %param.9) | copy-start | bytes 6148

commit v6 on v5

--- a/solution.py
+++ b/solution.py
@@ -217,7 +217,7 @@
             pltpu.VMEM((width, cols), own.dtype),
             pltpu.VMEM((rows.shape[0], cols), F32),
             pltpu.VMEM(shape, F32),
-            pltpu.SemaphoreType.DMA((4,)),
+            pltpu.SemaphoreType.DMA((2,)),
             pltpu.SemaphoreType.DMA((2, NY)),
         ],
         compiler_params=pltpu.CompilerParams(vmem_limit_bytes=32 * 1024 * 1024),

time: 128 us -> 128 us (level)
  no operation moved by 1% of the time
where the time goes in v6:
time: 128 us; the launch traced here: 127 us
  blocking collectives  93.6 us (73%)
  starting transfers between devices  24.2 us (19%)
  Pallas kernels  6.73 us (5%)
  waiting for transfers between devices  2.09 us (2%)
    all_to_all x3, blocking collectives, to_all(): return lax.all_to_all(copies, axes, 0, 0, tiled=True)  67.5 us
    all_gather x1, blocking collectives, on_device(): column = lax.all_gather(hidden, 'z')  26.1 us
    ppermute x1, starting transfers between devices, on_device(): partner_slabs = lax.ppermute(slabs, 'c', [(0, 1), (1, 0)])  10.5 us
    ppermute x1, starting transfers between devices, on_device(): partner_head = lax.ppermute(head, 'c', [(0, 1), (1, 0)])  8.91 us
    all_to_all x1, starting transfers between devices, on_device(): parts = lax.all_to_all(outgoing, ('y', 'x'), 0, 0, tiled=True)  4.74 us
    pallas_call x1, Pallas kernels, all_logits(): pl.pallas_call(logits_kernel, out_shape=jax.ShapeDtypeStruct(shape, F32),...  3.79 us
    pallas_call x3, Pallas kernels, call(): pl.pallas_call(kernel, out_shape=jax.ShapeDtypeStruct(shape, dtype), in_s...  2.94 us
  transfers between devices with their start and end apart: 3, of which 2 were waited for; matrix products, arithmetic and copies ran while one was open for 0% of the time, Pallas kernels for 0%

profile of v6, /device:TPU:1, one launch (start us, length us, event | category | flops | bytes accessed | tf_op | source)
XLA Modules:
  0.0 127.4 jit_solution(4956448854023012413)
XLA Ops:
  0.0 0.0 copy-start.5
  0.0 8.9 %collective-permute-start = (bf16[4096,512]{1,0:T(8,128)(2,1)}, bf16[4096,512]{1,0:T(8,128)(2,1)}, u32[]{:S(2)}, u32[]{:S(2)}) collective-permute-start(bf16[4096,512]{1,0:T(8,128)(2,1)} %own.1), channel_id=1, source_target_pairs={{0,4},{4,0},{1,5},{5,1},{2,6},{6,2},{3,7},{7,3},{8,12},{12,8},{9,1... | collective-permute-start | bytes 12582920 | tf_op jit(solution)/shard_map/ppermute | solution.py:238
  8.9 0.1 pad_add_fusion.place
  9.0 26.1 %all-gather.1 = bf16[16,4,4096]{2,1,0:T(4,128)(2,1)S(1)} all-gather(bf16[1,4,4096]{2,1,0:T(4,128)(2,1)} %bitcast.17), channel_id=2, replica_groups=mesh['y'=4,'z'=16,'c'=2,'x'=4] {'z'}, dimensions={0}, use_global_device_ids=true | all-gather | bytes 557056 | tf_op jit(solution)/shard_map/all_gather | solution.py:239
  35.1 0.3 copy.8
  35.4 0.0 copy-done.5
  35.4 0.2 broadcast_in_dim.6
  35.6 0.0 copy-start
  35.6 0.0 copy-start.1
  35.6 0.0 copy-start.2
  35.6 26.0 %all_to_all.20 = bf16[4,64,4608]{2,1,0:T(8,128)(2,1)S(1)} all-to-all(bf16[4,64,4608]{2,1,0:T(8,128)(2,1)S(1)} %broadcast_in_dim.6), channel_id=1, replica_groups=mesh['y'=4,'z'=16,'c'=2,'x'=4] {'y'}, dimensions={0} | all-to-all | bytes 4718592 | tf_op jit(solution)/shard_map/all_to_all | solution.py:229
  61.7 0.0 collective-permute-done.partner
  61.7 0.0 copy-done
  61.7 0.0 copy-done.1
  61.7 0.0 copy-done.2
  61.7 3.8 %shard_map.64 = f32[16,136,128]{2,1,0:T(8,128)} custom-call(bf16[256,4608]{1,0:T(8,128)(2,1)S(1)} %bitcast.14, bf16[4096,512]{1,0:T(8,128)(2,1)S(1)} %copy-done, bf16[4096,512]{1,0:T(8,128)(2,1)} %collective-permute-done.partner, bf16[4,4096]{1,0:T(4,128)(2,1)S(1)} %copy-done.2, bf16[64,4096]{1,0:T(8,128)(2,1)S(1)} %bitcast.16), custom_call_target="tpu_custom_call" | custom-call | tf_op jit(solution)/shard_map/pallas_call | solution.py:211
  65.5 0.0 copy-start.3
  65.5 4.7 %all-to-all-start.1 = ((f32[16,136,128]{2,1,0:T(8,128)}), f32[16,136,128]{2,1,0:T(8,128)S(1)}, u32[]{:S(2)}, u32[]{:S(2)}) async-start(f32[16,136,128]{2,1,0:T(8,128)} %shard_map.64), calls=%async_computation.1 | async-start | bytes 2228224 | tf_op jit(solution)/shard_map/all_to_all | solution.py:248
  70.3 10.5 %collective-permute-start.1 = (bf16[4,64,512]{2,1,0:T(8,128)(2,1)S(1)}, bf16[4,64,512]{2,1,0:T(8,128)(2,1)S(1)}, u32[]{:S(2)}, u32[]{:S(2)}) collective-permute-start(bf16[4,64,512]{2,1,0:T(8,128)(2,1)S(1)} %slice.4.slabs), channel_id=1, source_target_pairs={{0,4},{4,0},{1,5},{5,1},{2,6},{6,2},{3,7},{7,3},{8,12},{12,8},{9,1... | collective-permute-start | bytes 786440 | tf_op jit(solution)/shard_map/ppermute | solution.py:247
  80.8 1.1 collective-permute-done.1.partner_slabs
  81.9 1.0 all-to-all-done.1.parts
  82.9 0.0 copy-done.3
  82.9 0.0 copy-start.4
  82.9 1.1 shard_map.65
  84.0 18.7 %all_to_all.21.parts = bf16[16,16,256]{2,1,0:T(8,128)(2,1)S(1)} all-to-all(bf16[16,16,256]{2,1,0:T(8,128)(2,1)S(1)} %broadcast_in_dim.7), channel_id=1, replica_groups=mesh['y'=4,'z'=16,'c'=2,'x'=4] {'z'}, dimensions={0} | all-to-all | bytes 262144 | tf_op jit(solution)/shard_map/all_to_all | solution.py:229
  102.6 0.2 shard_map.66
  102.9 22.9 %all_to_all.22 = f32[32,16,128]{2,1,0:T(8,128)S(1)} all-to-all(f32[32,16,128]{2,1,0:T(8,128)S(1)} %broadcast_in_dim.8), channel_id=1, replica_groups=mesh['y'=4,'z'=16,'c'=2,'x'=4] {'y','c','x'}, dimensions={0} | all-to-all | bytes 524288 | tf_op jit(solution)/shard_map/all_to_all | solution.py:229
  125.7 0.0 copy-done.4
  125.7 1.7 %shard_map.67 = f32[8,4096]{1,0:T(8,128)} custom-call(s32[4,128]{1,0:T(4,128)S(1)} %bitcast.19, f32[512,128]{1,0:T(8,128)S(1)} %bitcast.15), custom_call_target="tpu_custom_call" | custom-call | tf_op jit(solution)/shard_map/pallas_call | solution.py:197
  (4 shorter events, 0.1 us)
Async XLA Ops:
  0.0 35.4 %copy-start.5 = (bf16[512,64]{0,1:T(8,128)(2,1)S(1)}, bf16[512,64]{0,1:T(8,128)(2,1)}, u32[]{:S(2)}) copy-start(bf16[512,64]{0,1:T(8,128)(2,1)} %param.10) | copy-start | bytes 196612
  0.0 61.7 %collective-permute-start = (bf16[4096,512]{1,0:T(8,128)(2,1)}, bf16[4096,512]{1,0:T(8,128)(2,1)}, u32[]{:S(2)}, u32[]{:S(2)}) collective-permute-start(bf16[4096,512]{1,0:T(8,128)(2,1)} %own.1), channel_id=1, source_target_pairs={{0,4},{4,0},{1,5},{5,1},{2,6},{6,2},{3,7},{7,3},{8,12},{12,8},{9,1... | collective-permute-start | bytes 12582920 | tf_op jit(solution)/shard_map/ppermute | solution.py:238
  35.6 26.1 %copy-start = (bf16[4096,512]{1,0:T(8,128)(2,1)S(1)}, bf16[4096,512]{1,0:T(8,128)(2,1)}, u32[]{:S(2)}) copy-start(bf16[4096,512]{1,0:T(8,128)(2,1)} %own.1) | copy-start | bytes 12582916
  35.6 26.1 %copy-start.1 = (bf16[4096,64]{0,1:T(8,128)(2,1)S(1)}, bf16[4096,64]{0,1:T(8,128)(2,1)}, u32[]{:S(2)}) copy-start(bf16[4096,64]{0,1:T(8,128)(2,1)} %param.11) | copy-start | bytes 1572868
  35.6 26.1 %copy-start.2 = (bf16[4,4096]{1,0:T(4,128)(2,1)S(1)}, bf16[4,4096]{1,0:T(4,128)(2,1)}, u32[]{:S(2)}) copy-start(bf16[4,4096]{1,0:T(4,128)(2,1)} %hidden) | copy-start | bytes 98308
  65.5 17.4 %copy-start.3 = (s32[512]{0:T(512)S(1)}, s32[512]{0:T(512)}, u32[]{:S(2)}) copy-start(s32[512]{0:T(512)} %param.8) | copy-start | bytes 6148
  65.5 17.4 %all-to-all-start.1 = ((f32[16,136,128]{2,1,0:T(8,128)}), f32[16,136,128]{2,1,0:T(8,128)S(1)}, u32[]{:S(2)}, u32[]{:S(2)}) async-start(f32[16,136,128]{2,1,0:T(8,128)} %shard_map.64), calls=%async_computation.1 | async-start | bytes 2228224 | tf_op jit(solution)/shard_map/all_to_all | solution.py:248
  70.3 11.7 %collective-permute-start.1 = (bf16[4,64,512]{2,1,0:T(8,128)(2,1)S(1)}, bf16[4,64,512]{2,1,0:T(8,128)(2,1)S(1)}, u32[]{:S(2)}, u32[]{:S(2)}) collective-permute-start(bf16[4,64,512]{2,1,0:T(8,128)(2,1)S(1)} %slice.4.slabs), channel_id=1, source_target_pairs={{0,4},{4,0},{1,5},{5,1},{2,6},{6,2},{3,7},{7,3},{8,12},{12,8},{9,1... | collective-permute-start | bytes 786440 | tf_op jit(solution)/shard_map/ppermute | solution.py:247
  82.9 42.8 %copy-start.4 = (s32[512]{0:T(512)S(1)}, s32[512]{0:T(512)}, u32[]{:S(2)}) copy-start(s32[512]{0:T(512)} %param.9) | copy-start | bytes 6148
